TPU v7x, 32 devices: a whole 2x2x4 slice. The times are simulated.
32 devices in a mesh: groups: 2 (over y), slab: 8 (over z, x), node: 2 (over core).
Axes of the slice: x: 2, y: 2, z: 4, core: 2. Of those that a mesh axis runs over, the one named last changes fastest.
Arguments:
- field_seeds: int32 [4], P(('groups', 'node')), parts along dimension 0, may hold values from 0 to 65520
- quad_weight: int32 [4], P('groups'), parts along dimension 0, may hold values from 1 to 9
- recharge: float32 [64, 64, 256], P(('groups', 'slab')), parts along dimension 0, may hold values from -16 to 16
- well_cells: int32 [128], P(('groups', 'slab')), parts along dimension 0, may hold values from 0 to 65535
- well_rates: float32 [128], P(('groups', 'slab')), parts along dimension 0, may hold values from -20 to 20
- sensitivity: float32 [64, 64, 256], P(('groups', 'slab')), parts along dimension 0, may hold values from -24 to 24
Outputs:
- head_field: float32 [4, 32, 64, 256], P(('groups', 'node'), 'slab'), parts along dimension 0
- adjoint_field: float32 [4, 32, 64, 256], P(('groups', 'node'), 'slab'), parts along dimension 0
- zone_gradient: float32 [16, 16, 64], P(('groups', 'slab')), parts along dimension 0
There are 2 independent parts, one for each index of `groups`. A program takes and returns all parts, laid end to end along the dimension named above; each array names one. Nothing has to cross between parts.
All inputs are finite; a program needn't handle non-finite values.
Results may differ from a plain program's by a relative error of at most 0.0003.
Values sent between devices are 32-bit elements; how exact they have to be, the bound alone decides.
A program may use at most 192 MiB of HBM per device.

v0:
```python
import jax
import jax.numpy as jnp
from jax import lax
from jax.sharding import PartitionSpec as P

LEVELS = 5
SWEEPS = 2
COARSE_SWEEPS = 8


OMEGA = 0.8


def with_halo(array, sides, width):
    for axis, dim in sides:
        peers, length = (lax.axis_size(axis), array.shape[dim])
        up = [(i, (i + 1) % peers) for i in range(peers - 1)]
        down = [(j, i) for i, j in up]
        last = lax.slice_in_dim(array, length - width, length, axis=dim)
        initial = lax.slice_in_dim(array, 0, width, axis=dim)
        before = lax.ppermute(last, axis, up)
        after = lax.ppermute(initial, axis, down)
        array = jnp.concatenate([before, array, after], axis=dim)
    return array


def log_conductivity(seed_value, width_x, width_y, width_z, x_start):
    extent = (width_x, width_y, width_z)
    index_x = lax.broadcasted_iota(jnp.int32, extent, 0) + x_start
    index_y = lax.broadcasted_iota(jnp.int32, extent, 1)
    index_z = lax.broadcasted_iota(jnp.int32, extent, 2)
    position = (index_x * width_y + index_y) * width_z + index_z
    hashed = position * 747796405 + seed_value * 277803737 + 1013904223
    hashed = jnp.bitwise_xor(
        hashed, lax.shift_right_logical(hashed, jnp.full(extent, 15, jnp.int32))
    )
    hashed = hashed * 1274126177
    hashed = jnp.bitwise_xor(
        hashed, lax.shift_right_logical(hashed, jnp.full(extent, 13, jnp.int32))
    )
    low_bits = jnp.bitwise_and(hashed, 65535)
    return 3.0 * (low_bits.astype(jnp.float32) / 65536.0) - 1.5


def restrict_all(values):
    leading = values.shape[:-3]
    width_x, width_y, width_z = values.shape[-3:]
    offset = len(leading)
    blocks = values.reshape(leading + (width_x // 2, 2, width_y // 2, 2, width_z // 2, 2))
    return jnp.sum(blocks, axis=(offset + 1, offset + 3, offset + 5)) * 0.125


def prolong_all(values):
    for axis_no in (-3, -2, -1):
        values = jnp.repeat(values, 2, axis=axis_no)
    return values


def build_operator(padded_logk, low_edge, high_edge, level_scale):
    center = padded_logk[1:-1]
    exp_center = jnp.exp(center)
    face_x = jnp.exp(0.5 * (padded_logk[:-1] + padded_logk[1:]))
    face_x = jnp.concatenate(
        [
            jnp.where(low_edge, 2.0 * exp_center[:1], face_x[:1]),
            face_x[1:-1],
            jnp.where(high_edge, 2.0 * exp_center[-1:], face_x[-1:]),
        ],
        0,
    )
    inner_y = jnp.exp(0.5 * (center[:, :-1] + center[:, 1:]))
    face_y = jnp.concatenate([2.0 * exp_center[:, :1], inner_y, 2.0 * exp_center[:, -1:]], 1)
    inner_z = jnp.exp(0.5 * (center[..., :-1] + center[..., 1:]))
    zeros_z = jnp.zeros_like(center[..., :1])
    face_up = jnp.concatenate([inner_z, zeros_z], 2)
    face_down = jnp.concatenate([zeros_z, inner_z], 2)
    diagonal = face_x[:-1] + face_x[1:] + face_y[:, :-1] + face_y[:, 1:] + face_down + face_up
    inverse = OMEGA / (level_scale * diagonal)
    return (face_x, face_y, face_up, face_down, diagonal, inverse, level_scale)


def apply_operator(operator_set, padded):
    face_x, face_y, face_up, face_down, diagonal, inverse, level_scale = operator_set
    values = padded[:, 1:-1]
    offdiag = face_x[:-1] * padded[:, :-2] + face_x[1:] * padded[:, 2:]
    zeros_y = jnp.zeros_like(values[:, :, :1])
    offdiag = offdiag + face_y[:, :-1] * jnp.concatenate([zeros_y, values[:, :, :-1]], 2)
    offdiag = offdiag + face_y[:, 1:] * jnp.concatenate([values[:, :, 1:], zeros_y], 2)
    zeros_z = jnp.zeros_like(values[..., :1])
    offdiag = offdiag + face_down * jnp.concatenate([zeros_z, values[..., :-1]], 3)
    offdiag = offdiag + face_up * jnp.concatenate([values[..., 1:], zeros_z], 3)
    return level_scale * (diagonal * values - offdiag)


def vcycle(level_at, source, operators, pad_fn, coarse_fn):
    operator_set = operators[level_at]
    inverse = operator_set[5]
    iterate = inverse * source
    if level_at == LEVELS - 1:
        for sweep_no in range(COARSE_SWEEPS - 1):
            iterate = iterate + inverse * (source - apply_operator(operator_set, pad_fn(iterate)))
        return iterate
    iterate = iterate + inverse * (source - apply_operator(operator_set, pad_fn(iterate)))
    residue = source - apply_operator(operator_set, pad_fn(iterate))
    iterate = iterate + coarse_fn(level_at, residue)
    for sweep_no in range(SWEEPS):
        iterate = iterate + inverse * (source - apply_operator(operator_set, pad_fn(iterate)))
    return iterate


def zero_pad(values):
    return jnp.pad(values, ((0, 0), (1, 1), (0, 0), (0, 0)))


def cell_gradient(operator_set, head_pad, adj_pad, low_edge, high_edge):
    face_x, face_y, face_up = (operator_set[0], operator_set[1], operator_set[2])
    heads_in = head_pad[1:-1]
    adj_in = adj_pad[1:-1]
    width_x, width_y = (heads_in.shape[0], heads_in.shape[1])
    ones_cell = jnp.ones((1, 1, 1), head_pad.dtype)
    prod_x = face_x * (head_pad[:-1] - head_pad[1:]) * (adj_pad[:-1] - adj_pad[1:])
    weight_x = jnp.concatenate(
        [
            jnp.where(low_edge, 1.0, 0.5) * ones_cell,
            jnp.full((width_x - 1, 1, 1), 0.5, dtype=head_pad.dtype),
            jnp.where(high_edge, 1.0, 0.5) * ones_cell,
        ],
        0,
    )
    prod_x = prod_x * weight_x
    grad_x = prod_x[:-1] + prod_x[1:]
    zeros_y = jnp.zeros_like(heads_in[:, :1])
    head_y = jnp.concatenate([zeros_y, heads_in, zeros_y], 1)
    adj_y = jnp.concatenate([zeros_y, adj_in, zeros_y], 1)
    prod_y = face_y * (head_y[:, :-1] - head_y[:, 1:]) * (adj_y[:, :-1] - adj_y[:, 1:])
    weight_y = jnp.concatenate(
        [ones_cell, jnp.full((1, width_y - 1, 1), 0.5, dtype=head_pad.dtype), ones_cell], 1
    )
    prod_y = prod_y * weight_y
    grad_y = prod_y[:, :-1] + prod_y[:, 1:]
    zeros_z = jnp.zeros_like(heads_in[..., :1])
    up_head = jnp.concatenate([heads_in[..., 1:], zeros_z], 2)
    up_adj = jnp.concatenate([adj_in[..., 1:], zeros_z], 2)
    prod_z = face_up * (heads_in - up_head) * (adj_in - up_adj)
    grad_z = 0.5 * (prod_z + jnp.concatenate([zeros_z, prod_z[..., :-1]], 2))
    return -(grad_x + grad_y + grad_z)


def zone_total(cells):
    width_x, width_y, width_z = cells.shape
    blocks = cells.reshape(width_x // 4, 4, width_y // 4, 4, width_z // 4, 4)
    return jnp.sum(blocks, axis=(1, 3, 5))


def body(field_seeds, quad_weight, recharge, well_cells, well_rates, sensitivity):
    slab_index = lax.axis_index("slab")
    slab_count = lax.axis_size("slab")
    low_edge = slab_index == 0
    high_edge = slab_index == slab_count - 1
    width_x, width_y, width_z = recharge.shape
    log_cond = log_conductivity(field_seeds[0], width_x, width_y, width_z, slab_index * width_x)
    merge_depth = 2
    local_logk = [log_cond]
    for level_at in range(1, 3):
        local_logk.append(restrict_all(local_logk[-1]))
    operators = []
    for level_at in range(merge_depth):
        padded_logk = with_halo(local_logk[level_at], (("slab", 0),), 1)
        operators.append(build_operator(padded_logk, low_edge, high_edge, 0.25**level_at))
    coarse_logk = lax.all_gather(local_logk[2], "slab", axis=0, tiled=True)
    for level_at in range(merge_depth, LEVELS):
        padded = jnp.pad(coarse_logk, ((1, 1), (0, 0), (0, 0)))
        operators.append(build_operator(padded, True, True, 0.25**level_at))
        if level_at + 1 < LEVELS:
            coarse_logk = restrict_all(coarse_logk)

    def halo_pad(values):
        return with_halo(values, (("slab", 1),), 1)

    def level_solve(level_at, source):
        return vcycle(level_at, source, operators, halo_pad, spread_coarse)

    def merged_coarse(level_at, residue):
        return prolong_all(
            vcycle(level_at + 1, restrict_all(residue), operators, zero_pad, merged_coarse)
        )

    def spread_coarse(level_at, residue):
        if level_at + 1 < merge_depth:
            return prolong_all(level_solve(level_at + 1, restrict_all(residue)))
        coarse_source = restrict_all(residue)
        whole_source = lax.all_gather(coarse_source, "slab", axis=1, tiled=True)
        whole_fix = vcycle(level_at + 1, whole_source, operators, zero_pad, merged_coarse)
        plane_count = coarse_source.shape[1]
        own_fix = lax.dynamic_slice_in_dim(whole_fix, slab_index * plane_count, plane_count, 1)
        return prolong_all(own_fix)

    source = (
        recharge.reshape(-1).at[well_cells].add(well_rates).reshape(1, width_x, width_y, width_z)
    )
    paired = level_solve(0, jnp.concatenate([source, sensitivity[None]], 0))
    head_field = paired[:1]
    adjoint_field = paired[1:]
    both_pad = with_halo(jnp.concatenate([head_field, adjoint_field], 0), (("slab", 1),), 1)
    cells = cell_gradient(operators[0], both_pad[0], both_pad[1], low_edge, high_edge)
    weights = quad_weight.astype(jnp.float32)
    node_index = lax.axis_index("node")
    own_weight = jnp.sum(
        jnp.where(jnp.arange(weights.shape[0], dtype=jnp.int32) == node_index, weights, 0.0)
    )
    portion = own_weight / jnp.sum(weights)
    zone_gradient = lax.psum(portion * zone_total(cells), "node")
    return (head_field, adjoint_field, zone_gradient)


def solution(mesh):
    placed = (
        P(("groups", "node")),
        P("groups"),
        P(("groups", "slab"), None, None),
        P(("groups", "slab")),
        P(("groups", "slab")),
        P(("groups", "slab"), None, None),
    )
    return jax.shard_map(
        body,
        mesh=mesh,
        in_specs=placed,
        out_specs=(
            P(("groups", "node"), "slab", None, None),
            P(("groups", "node"), "slab", None, None),
            P(("groups", "slab"), None, None),
        ),
        check_vma=False,
    )
```

profile of v0, /device:TPU:0, one launch (start us, length us, event | category | flops | bytes accessed | tf_op | source)
XLA Modules:
  0.0 269.3 jit_solution(14466750963269581465)
XLA Ops:
  2.9 5.5 %collective-permute-start = (f32[1,64,256]{2,1,0:T(8,128)}, f32[1,64,256]{2,1,0:T(8,128)}, u32[]{:S(2)}, u32[]{:S(2)}) collective-permute-start(f32[1,64,256]{2,1,0:T(8,128)} %get-tuple-element.66), channel_id=1, source_target_pairs={{0,2},{2,4},{4,6},{6,8},{8,10},{10,12},{12,14},{1,3},{3,5},{5,7},{... | collective-permute-start | bytes 196616 | tf_op jit(solution)/shard_map/ppermute | solution.py:21
  8.3 1.3 collective-permute-start.1
  10.5 5.1 %collective-permute-start.6 = (f32[1,32,128]{2,1,0:T(8,128)}, f32[1,32,128]{2,1,0:T(8,128)}, u32[]{:S(2)}, u32[]{:S(2)}) collective-permute-start(f32[1,32,128]{2,1,0:T(8,128)} %get-tuple-element.145), channel_id=1, source_target_pairs={{0,2},{2,4},{4,6},{6,8},{8,10},{10,12},{12,14},{1,3},{3,5},{5,7},{... | collective-permute-start | bytes 49160 | tf_op jit(solution)/shard_map/ppermute | solution.py:21
  15.6 1.3 collective-permute-start.7
  18.5 1.0 reduce_sum.123
  19.7 32.6 %all-gather = f32[128,64]{1,0:T(8,128)S(1)} all-gather(f32[16,64]{1,0:T(8,128)S(1)} %broadcast_multiply_fusion.11), channel_id=2, replica_groups=mesh['groups'=2,'slab'=8,'node'=2] {'slab'}, dimensions={0}, use_global_device_ids=true | all-gather | bytes 36864 | tf_op jit(solution)/shard_map/all_gather | solution.py:170
  54.4 2.1 reshape.163
  63.2 1.3 convert_reduce_fusion
  64.5 1.5 multiply_divide_fusion
  73.0 2.8 %collective-permute-start.2 = (f32[2,1,64,256]{3,2,1,0:T(8,128)S(1)}, f32[2,1,64,256]{3,2,1,0:T(8,128)S(1)}, u32[]{:S(2)}, u32[]{:S(2)}) collective-permute-start(f32[2,1,64,256]{3,2,1,0:T(8,128)S(1)} %get-tuple-element.56), channel_id=1, source_target_pairs={{0,2},{2,4},{4,6},{6,8},{8,10},{10,12},{12,14},{1,3},{3,5},{5,7},{... | collective-permute-start | bytes 393224 | tf_op jit(solution)/shard_map/ppermute | solution.py:21
  75.8 1.3 collective-permute-start.3
  77.3 1.3 collective-permute-done.2
  78.6 4.7 %collective-permute-done.3 = f32[2,1,64,256]{3,2,1,0:T(8,128)S(1)} collective-permute-done((f32[2,1,64,256]{3,2,1,0:T(8,128)S(1)}, f32[2,1,64,256]{3,2,1,0:T(8,128)S(1)}, u32[]{:S(2)}, u32[]{:S(2)}) %collective-permute-start.3) | collective-permute-done | bytes 131104 | tf_op jit(solution)/shard_map/ppermute | solution.py:22
  84.0 2.5 collective-permute-start.4
  86.5 1.3 collective-permute-start.5
  88.0 1.0 collective-permute-done.4
  89.0 4.4 %collective-permute-done.5 = f32[2,1,64,256]{3,2,1,0:T(8,128)S(1)} collective-permute-done((f32[2,1,64,256]{3,2,1,0:T(8,128)S(1)}, f32[2,1,64,256]{3,2,1,0:T(8,128)S(1)}, u32[]{:S(2)}, u32[]{:S(2)}) %collective-permute-start.5) | collective-permute-done | bytes 131104 | tf_op jit(solution)/shard_map/ppermute | solution.py:22
  94.0 34.8 %reshape.161 = f32[2,2,2,32,2,128,2]{6,5,4,3,2,1,0:T(8,128)} reshape(f32[2,4,64,256]{3,2,1,0:T(8,128)S(1)} %fusion.29) | data formatting | bytes 1048576 | tf_op jit(solution)/shard_map/reshape | solution.py:49
  128.8 12.2 %reduce_sum.120 = f32[2,2,32,128]{3,2,1,0:T(8,128)S(1)} reduce(f32[2,2,2,32,2,128,2]{6,5,4,3,2,1,0:T(8,128)} %reshape.161, f32[]{:T(128)} %constant.49.clone.1), dimensions={2,4,6}, to_apply=%region_1.0 | reduce | flops 114688 | bytes 589828 | tf_op jit(solution)/shard_map/reduce_sum | solution.py:50
  141.1 4.6 %collective-permute-start.8 = (f32[2,1,32,128]{3,2,1,0:T(8,128)S(1)}, f32[2,1,32,128]{3,2,1,0:T(8,128)S(1)}, u32[]{:S(2)}, u32[]{:S(2)}) collective-permute-start(f32[2,1,32,128]{3,2,1,0:T(8,128)S(1)} %get-tuple-element.116), channel_id=1, source_target_pairs={{0,2},{2,4},{4,6},{6,8},{8,10},{10,12},{12,14},{1,3},{3,5},{5,7},{... | collective-permute-start | bytes 98312 | tf_op jit(solution)/shard_map/ppermute | solution.py:21
  145.8 1.3 collective-permute-start.9
  147.3 4.2 %collective-permute-done.9 = f32[2,1,32,128]{3,2,1,0:T(8,128)S(1)} collective-permute-done((f32[2,1,32,128]{3,2,1,0:T(8,128)S(1)}, f32[2,1,32,128]{3,2,1,0:T(8,128)S(1)}, u32[]{:S(2)}, u32[]{:S(2)}) %collective-permute-start.9) | collective-permute-done | bytes 32800 | tf_op jit(solution)/shard_map/ppermute | solution.py:22
  151.7 2.8 %collective-permute-start.10 = (f32[2,1,32,128]{3,2,1,0:T(8,128)S(1)}, f32[2,1,32,128]{3,2,1,0:T(8,128)S(1)}, u32[]{:S(2)}, u32[]{:S(2)}) collective-permute-start(f32[2,1,32,128]{3,2,1,0:T(8,128)S(1)} %get-tuple-element.110), channel_id=1, source_target_pairs={{0,2},{2,4},{4,6},{6,8},{8,10},{10,12},{12,14},{1,3},{3,5},{5,7},{... | collective-permute-start | bytes 98312 | tf_op jit(solution)/shard_map/ppermute | solution.py:21
  154.5 1.3 collective-permute-start.11
  156.1 4.3 %collective-permute-done.11 = f32[2,1,32,128]{3,2,1,0:T(8,128)S(1)} collective-permute-done((f32[2,1,32,128]{3,2,1,0:T(8,128)S(1)}, f32[2,1,32,128]{3,2,1,0:T(8,128)S(1)}, u32[]{:S(2)}, u32[]{:S(2)}) %collective-permute-start.11) | collective-permute-done | bytes 32800 | tf_op jit(solution)/shard_map/ppermute | solution.py:22
  161.2 2.8 %reduce_sum.126 = f32[2,16,2,64,2]{4,3,2,1,0:T(8,128)S(1)} reshape(f32[2,32,128]{2,1,0:T(8,128)} %fusion.148) | data formatting | bytes 65536 | tf_op jit(solution)/shard_map/reduce_sum | solution.py:50
  165.8 30.7 %all-gather.1 = f32[2,128,64]{2,1,0:T(8,128)S(1)} all-gather(f32[2,16,64]{2,1,0:T(8,128)S(1)} %broadcast_multiply_fusion.8), channel_id=3, replica_groups=mesh['groups'=2,'slab'=8,'node'=2] {'slab'}, dimensions={1}, use_global_device_ids=true | all-gather | bytes 73728 | tf_op jit(solution)/shard_map/all_gather | solution.py:192
  197.4 1.2 fusion.84
  199.0 5.7 %reshape.162 = f32[2,4,2,8,2,32,2]{6,5,4,3,2,1,0:T(8,128)} reshape(f32[2,8,16,64]{3,2,1,0:T(8,128)S(1)} %fusion.94) | data formatting | bytes 131072 | tf_op jit(solution)/shard_map/reshape | solution.py:49
  204.7 2.6 reduce_sum.128
  211.8 1.4 collective-permute-start.12
  213.2 1.3 collective-permute-start.13
  215.4 3.6 %collective-permute-done.13 = f32[2,1,32,128]{3,2,1,0:T(8,128)S(1)} collective-permute-done((f32[2,1,32,128]{3,2,1,0:T(8,128)S(1)}, f32[2,1,32,128]{3,2,1,0:T(8,128)S(1)}, u32[]{:S(2)}, u32[]{:S(2)}) %collective-permute-start.13) | collective-permute-done | bytes 32800 | tf_op jit(solution)/shard_map/ppermute | solution.py:22
  219.2 3.5 %collective-permute-start.14 = (f32[2,1,32,128]{3,2,1,0:T(8,128)S(1)}, f32[2,1,32,128]{3,2,1,0:T(8,128)S(1)}, u32[]{:S(2)}, u32[]{:S(2)}) collective-permute-start(f32[2,1,32,128]{3,2,1,0:T(8,128)S(1)} %get-tuple-element.89), channel_id=1, source_target_pairs={{0,2},{2,4},{4,6},{6,8},{8,10},{10,12},{12,14},{1,3},{3,5},{5,7},{... | collective-permute-start | bytes 98312 | tf_op jit(solution)/shard_map/ppermute | solution.py:21
  222.7 1.3 collective-permute-start.15
  224.3 4.2 %collective-permute-done.15 = f32[2,1,32,128]{3,2,1,0:T(8,128)S(1)} collective-permute-done((f32[2,1,32,128]{3,2,1,0:T(8,128)S(1)}, f32[2,1,32,128]{3,2,1,0:T(8,128)S(1)}, u32[]{:S(2)}, u32[]{:S(2)}) %collective-permute-start.15) | collective-permute-done | bytes 32800 | tf_op jit(solution)/shard_map/ppermute | solution.py:22
  229.9 3.0 %collective-permute-start.16 = (f32[2,1,64,256]{3,2,1,0:T(8,128)S(1)}, f32[2,1,64,256]{3,2,1,0:T(8,128)S(1)}, u32[]{:S(2)}, u32[]{:S(2)}) collective-permute-start(f32[2,1,64,256]{3,2,1,0:T(8,128)S(1)} %get-tuple-element.44), channel_id=1, source_target_pairs={{0,2},{2,4},{4,6},{6,8},{8,10},{10,12},{12,14},{1,3},{3,5},{5,7},{... | collective-permute-start | bytes 393224 | tf_op jit(solution)/shard_map/ppermute | solution.py:21
  232.9 1.3 collective-permute-start.17
  234.4 1.0 collective-permute-done.16
  235.4 4.4 %collective-permute-done.17 = f32[2,1,64,256]{3,2,1,0:T(8,128)S(1)} collective-permute-done((f32[2,1,64,256]{3,2,1,0:T(8,128)S(1)}, f32[2,1,64,256]{3,2,1,0:T(8,128)S(1)}, u32[]{:S(2)}, u32[]{:S(2)}) %collective-permute-start.17) | collective-permute-done | bytes 131104 | tf_op jit(solution)/shard_map/ppermute | solution.py:22
  240.5 3.7 %collective-permute-start.18 = (f32[2,1,64,256]{3,2,1,0:T(8,128)S(1)}, f32[2,1,64,256]{3,2,1,0:T(8,128)S(1)}, u32[]{:S(2)}, u32[]{:S(2)}) collective-permute-start(f32[2,1,64,256]{3,2,1,0:T(8,128)S(1)} %get-tuple-element.38), channel_id=1, source_target_pairs={{0,2},{2,4},{4,6},{6,8},{8,10},{10,12},{12,14},{1,3},{3,5},{5,7},{... | collective-permute-start | bytes 393224 | tf_op jit(solution)/shard_map/ppermute | solution.py:21
  244.3 1.3 collective-permute-start.19
  246.8 4.4 %collective-permute-done.19 = f32[2,1,64,256]{3,2,1,0:T(8,128)S(1)} collective-permute-done((f32[2,1,64,256]{3,2,1,0:T(8,128)S(1)}, f32[2,1,64,256]{3,2,1,0:T(8,128)S(1)}, u32[]{:S(2)}, u32[]{:S(2)}) %collective-permute-start.19) | collective-permute-done | bytes 131104 | tf_op jit(solution)/shard_map/ppermute | solution.py:22
  252.2 4.5 %collective-permute-start.20 = (f32[2,1,64,256]{3,2,1,0:T(8,128)S(1)}, f32[2,1,64,256]{3,2,1,0:T(8,128)S(1)}, u32[]{:S(2)}, u32[]{:S(2)}) collective-permute-start(f32[2,1,64,256]{3,2,1,0:T(8,128)S(1)} %get-tuple-element.30), channel_id=1, source_target_pairs={{0,2},{2,4},{4,6},{6,8},{8,10},{10,12},{12,14},{1,3},{3,5},{5,7},{... | collective-permute-start | bytes 393224 | tf_op jit(solution)/shard_map/ppermute | solution.py:21
  256.7 1.3 collective-permute-start.21
  259.2 4.4 %collective-permute-done.21 = f32[2,1,64,256]{3,2,1,0:T(8,128)S(1)} collective-permute-done((f32[2,1,64,256]{3,2,1,0:T(8,128)S(1)}, f32[2,1,64,256]{3,2,1,0:T(8,128)S(1)}, u32[]{:S(2)}, u32[]{:S(2)}) %collective-permute-start.21) | collective-permute-done | bytes 131104 | tf_op jit(solution)/shard_map/ppermute | solution.py:22
  263.8 2.1 reduce_sum.135
  266.2 3.1 %psum.7 = f32[1,16,64]{2,1,0:T(8,128)} all-reduce(f32[1,16,64]{2,1,0:T(8,128)S(1)} %multiply_bitcast_fusion), channel_id=1, replica_groups=mesh['groups'=2,'slab'=8,'node'=2] {'node'}, use_global_device_ids=true, to_apply=%region_15.16 | all-reduce | flops 1024 | bytes 8192 | tf_op jit(solution)/shard_map/psum | solution.py:212
  (371 shorter events, 35.3 us)
Async XLA Ops:
  2.9 67.8 %collective-permute-start = (f32[1,64,256]{2,1,0:T(8,128)}, f32[1,64,256]{2,1,0:T(8,128)}, u32[]{:S(2)}, u32[]{:S(2)}) collective-permute-start(f32[1,64,256]{2,1,0:T(8,128)} %get-tuple-element.66), channel_id=1, source_target_pairs={{0,2},{2,4},{4,6},{6,8},{8,10},{10,12},{12,14},{1,3},{3,5},{5,7},{... | collective-permute-start | bytes 196616 | tf_op jit(solution)/shard_map/ppermute | solution.py:21
  8.3 62.4 %collective-permute-start.1 = (f32[1,64,256]{2,1,0:T(8,128)}, f32[1,64,256]{2,1,0:T(8,128)}, u32[]{:S(2)}, u32[]{:S(2)}) collective-permute-start(f32[1,64,256]{2,1,0:T(8,128)} %get-tuple-element.65), channel_id=1, source_target_pairs={{2,0},{4,2},{6,4},{8,6},{10,8},{12,10},{14,12},{3,1},{5,3},{7,5},{... | collective-permute-start | bytes 196616 | tf_op jit(solution)/shard_map/ppermute | solution.py:22
  9.9 48.5 %copy-start.73 = (f32[2,32,128]{2,1,0:T(8,128)}, f32[2,32,128]{2,1,0:T(8,128)S(1)}, u32[]{:S(2)}) copy-start(f32[2,32,128]{2,1,0:T(8,128)S(1)} %get-tuple-element.136) | copy-start | bytes 98308
  10.5 59.1 %collective-permute-start.6 = (f32[1,32,128]{2,1,0:T(8,128)}, f32[1,32,128]{2,1,0:T(8,128)}, u32[]{:S(2)}, u32[]{:S(2)}) collective-permute-start(f32[1,32,128]{2,1,0:T(8,128)} %get-tuple-element.145), channel_id=1, source_target_pairs={{0,2},{2,4},{4,6},{6,8},{8,10},{10,12},{12,14},{1,3},{3,5},{5,7},{... | collective-permute-start | bytes 49160 | tf_op jit(solution)/shard_map/ppermute | solution.py:21
  15.6 54.0 %collective-permute-start.7 = (f32[1,32,128]{2,1,0:T(8,128)}, f32[1,32,128]{2,1,0:T(8,128)}, u32[]{:S(2)}, u32[]{:S(2)}) collective-permute-start(f32[1,32,128]{2,1,0:T(8,128)} %get-tuple-element.144), channel_id=1, source_target_pairs={{2,0},{4,2},{6,4},{8,6},{10,8},{12,10},{14,12},{3,1},{5,3},{7,5},{... | collective-permute-start | bytes 49160 | tf_op jit(solution)/shard_map/ppermute | solution.py:22
  17.1 55.0 %copy-start.14 = (f32[4,64,255]{2,1,0:T(8,128)}, f32[4,64,255]{2,1,0:T(8,128)S(1)}, u32[]{:S(2)}) copy-start(f32[4,64,255]{2,1,0:T(8,128)S(1)} %fusion.70) | copy-start | bytes 783364
  17.1 54.6 %copy-start.20 = (f32[4,63,256]{2,1,0:T(8,128)}, f32[4,63,256]{2,1,0:T(8,128)S(1)}, u32[]{:S(2)}) copy-start(f32[4,63,256]{2,1,0:T(8,128)S(1)} %fusion.72) | copy-start | bytes 774148
  57.2 13.2 %copy-start.64 = (f32[2,32,127]{2,1,0:T(8,128)S(1)}, f32[2,32,127]{2,1,0:T(8,128)}, u32[]{:S(2)}) copy-start(f32[2,32,127]{2,1,0:T(8,128)} %fusion.217) | copy-start | bytes 97540
  58.3 13.5 %copy-start.77 = (f32[4,1,256]{2,1,0:T(1,128)}, f32[4,1,256]{2,1,0:T(1,128)S(1)}, u32[]{:S(2)}) copy-start(f32[4,1,256]{2,1,0:T(1,128)S(1)} %get-tuple-element.63) | copy-start | bytes 12292
  58.3 13.5 %copy-start.79 = (f32[4,1,256]{2,1,0:T(1,128)}, f32[4,1,256]{2,1,0:T(1,128)S(1)}, u32[]{:S(2)}) copy-start(f32[4,1,256]{2,1,0:T(1,128)S(1)} %get-tuple-element.64) | copy-start | bytes 12292
  70.5 89.9 %copy-start.28 = (f32[2,32,128]{2,1,0:T(8,128)}, f32[2,32,128]{2,1,0:T(8,128)S(1)}, u32[]{:S(2)}) copy-start(f32[2,32,128]{2,1,0:T(8,128)S(1)} %get-tuple-element.21) | copy-start | bytes 98308
  70.5 89.9 %copy-start.30 = (f32[2,32,128]{2,1,0:T(8,128)}, f32[2,32,128]{2,1,0:T(8,128)S(1)}, u32[]{:S(2)}) copy-start(f32[2,32,128]{2,1,0:T(8,128)S(1)} %get-tuple-element.22) | copy-start | bytes 98308
  70.5 89.9 %copy-start.40 = (f32[2,32,128]{2,1,0:T(8,128)}, f32[2,32,128]{2,1,0:T(8,128)S(1)}, u32[]{:S(2)}) copy-start(f32[2,32,128]{2,1,0:T(8,128)S(1)} %get-tuple-element.20) | copy-start | bytes 98308
  70.5 89.9 %copy-start.42 = (f32[2,32,128]{2,1,0:T(8,128)}, f32[2,32,128]{2,1,0:T(8,128)S(1)}, u32[]{:S(2)}) copy-start(f32[2,32,128]{2,1,0:T(8,128)S(1)} %get-tuple-element.138) | copy-start | bytes 98308
  70.5 89.9 %copy-start.44 = (f32[2,32,128]{2,1,0:T(8,128)}, f32[2,32,128]{2,1,0:T(8,128)S(1)}, u32[]{:S(2)}) copy-start(f32[2,32,128]{2,1,0:T(8,128)S(1)} %get-tuple-element.139) | copy-start | bytes 98308
  70.5 89.9 %copy-start.46 = (f32[2,32,128]{2,1,0:T(8,128)}, f32[2,32,128]{2,1,0:T(8,128)S(1)}, u32[]{:S(2)}) copy-start(f32[2,32,128]{2,1,0:T(8,128)S(1)} %get-tuple-element.140) | copy-start | bytes 98308
  70.6 80.9 %copy-start.53 = (f32[2,32,128]{2,1,0:T(8,128)}, f32[2,32,128]{2,1,0:T(8,128)S(1)}, u32[]{:S(2)}) copy-start(f32[2,32,128]{2,1,0:T(8,128)S(1)} %get-tuple-element.24) | copy-start | bytes 98308
  70.7 89.8 %copy-start.48 = (f32[2,32,128]{2,1,0:T(8,128)}, f32[2,32,128]{2,1,0:T(8,128)S(1)}, u32[]{:S(2)}) copy-start(f32[2,32,128]{2,1,0:T(8,128)S(1)} %get-tuple-element.141) | copy-start | bytes 98308
  72.0 21.4 %copy-start.2 = (f32[4,64,256]{2,1,0:T(8,128)}, f32[4,64,256]{2,1,0:T(8,128)S(1)}, u32[]{:S(2)}) copy-start(f32[4,64,256]{2,1,0:T(8,128)S(1)} %get-tuple-element.25) | copy-start | bytes 786436
  72.0 21.4 %copy-start.4 = (f32[4,64,256]{2,1,0:T(8,128)}, f32[4,64,256]{2,1,0:T(8,128)S(1)}, u32[]{:S(2)}) copy-start(f32[4,64,256]{2,1,0:T(8,128)S(1)} %get-tuple-element.58) | copy-start | bytes 786436
  72.0 21.4 %copy-start.6 = (f32[4,64,256]{2,1,0:T(8,128)}, f32[4,64,256]{2,1,0:T(8,128)S(1)}, u32[]{:S(2)}) copy-start(f32[4,64,256]{2,1,0:T(8,128)S(1)} %get-tuple-element.59) | copy-start | bytes 786436
  72.0 21.4 %copy-start.8 = (f32[4,64,256]{2,1,0:T(8,128)}, f32[4,64,256]{2,1,0:T(8,128)S(1)}, u32[]{:S(2)}) copy-start(f32[4,64,256]{2,1,0:T(8,128)S(1)} %get-tuple-element.60) | copy-start | bytes 786436
  72.3 21.1 %copy-start.10 = (f32[4,64,256]{2,1,0:T(8,128)}, f32[4,64,256]{2,1,0:T(8,128)S(1)}, u32[]{:S(2)}) copy-start(f32[4,64,256]{2,1,0:T(8,128)S(1)} %get-tuple-element.61) | copy-start | bytes 786436
  73.0 5.6 %collective-permute-start.2 = (f32[2,1,64,256]{3,2,1,0:T(8,128)S(1)}, f32[2,1,64,256]{3,2,1,0:T(8,128)S(1)}, u32[]{:S(2)}, u32[]{:S(2)}) collective-permute-start(f32[2,1,64,256]{3,2,1,0:T(8,128)S(1)} %get-tuple-element.56), channel_id=1, source_target_pairs={{0,2},{2,4},{4,6},{6,8},{8,10},{10,12},{12,14},{1,3},{3,5},{5,7},{... | collective-permute-start | bytes 393224 | tf_op jit(solution)/shard_map/ppermute | solution.py:21
  75.8 7.5 %collective-permute-start.3 = (f32[2,1,64,256]{3,2,1,0:T(8,128)S(1)}, f32[2,1,64,256]{3,2,1,0:T(8,128)S(1)}, u32[]{:S(2)}, u32[]{:S(2)}) collective-permute-start(f32[2,1,64,256]{3,2,1,0:T(8,128)S(1)} %get-tuple-element.57), channel_id=1, source_target_pairs={{2,0},{4,2},{6,4},{8,6},{10,8},{12,10},{14,12},{3,1},{5,3},{7,5},{... | collective-permute-start | bytes 393224 | tf_op jit(solution)/shard_map/ppermute | solution.py:22
  84.0 5.0 %collective-permute-start.4 = (f32[2,1,64,256]{3,2,1,0:T(8,128)S(1)}, f32[2,1,64,256]{3,2,1,0:T(8,128)S(1)}, u32[]{:S(2)}, u32[]{:S(2)}) collective-permute-start(f32[2,1,64,256]{3,2,1,0:T(8,128)S(1)} %get-tuple-element.50), channel_id=1, source_target_pairs={{0,2},{2,4},{4,6},{6,8},{8,10},{10,12},{12,14},{1,3},{3,5},{5,7},{... | collective-permute-start | bytes 393224 | tf_op jit(solution)/shard_map/ppermute | solution.py:21
  86.5 6.9 %collective-permute-start.5 = (f32[2,1,64,256]{3,2,1,0:T(8,128)S(1)}, f32[2,1,64,256]{3,2,1,0:T(8,128)S(1)}, u32[]{:S(2)}, u32[]{:S(2)}) collective-permute-start(f32[2,1,64,256]{3,2,1,0:T(8,128)S(1)} %get-tuple-element.51), channel_id=1, source_target_pairs={{2,0},{4,2},{6,4},{8,6},{10,8},{12,10},{14,12},{3,1},{5,3},{7,5},{... | collective-permute-start | bytes 393224 | tf_op jit(solution)/shard_map/ppermute | solution.py:22
  141.1 6.2 %collective-permute-start.8 = (f32[2,1,32,128]{3,2,1,0:T(8,128)S(1)}, f32[2,1,32,128]{3,2,1,0:T(8,128)S(1)}, u32[]{:S(2)}, u32[]{:S(2)}) collective-permute-start(f32[2,1,32,128]{3,2,1,0:T(8,128)S(1)} %get-tuple-element.116), channel_id=1, source_target_pairs={{0,2},{2,4},{4,6},{6,8},{8,10},{10,12},{12,14},{1,3},{3,5},{5,7},{... | collective-permute-start | bytes 98312 | tf_op jit(solution)/shard_map/ppermute | solution.py:21
  145.8 5.8 %collective-permute-start.9 = (f32[2,1,32,128]{3,2,1,0:T(8,128)S(1)}, f32[2,1,32,128]{3,2,1,0:T(8,128)S(1)}, u32[]{:S(2)}, u32[]{:S(2)}) collective-permute-start(f32[2,1,32,128]{3,2,1,0:T(8,128)S(1)} %get-tuple-element.117), channel_id=1, source_target_pairs={{2,0},{4,2},{6,4},{8,6},{10,8},{12,10},{14,12},{3,1},{5,3},{7,5},{... | collective-permute-start | bytes 98312 | tf_op jit(solution)/shard_map/ppermute | solution.py:22
  151.7 4.4 %collective-permute-start.10 = (f32[2,1,32,128]{3,2,1,0:T(8,128)S(1)}, f32[2,1,32,128]{3,2,1,0:T(8,128)S(1)}, u32[]{:S(2)}, u32[]{:S(2)}) collective-permute-start(f32[2,1,32,128]{3,2,1,0:T(8,128)S(1)} %get-tuple-element.110), channel_id=1, source_target_pairs={{0,2},{2,4},{4,6},{6,8},{8,10},{10,12},{12,14},{1,3},{3,5},{5,7},{... | collective-permute-start | bytes 98312 | tf_op jit(solution)/shard_map/ppermute | solution.py:21
  154.5 5.9 %collective-permute-start.11 = (f32[2,1,32,128]{3,2,1,0:T(8,128)S(1)}, f32[2,1,32,128]{3,2,1,0:T(8,128)S(1)}, u32[]{:S(2)}, u32[]{:S(2)}) collective-permute-start(f32[2,1,32,128]{3,2,1,0:T(8,128)S(1)} %get-tuple-element.111), channel_id=1, source_target_pairs={{2,0},{4,2},{6,4},{8,6},{10,8},{12,10},{14,12},{3,1},{5,3},{7,5},{... | collective-permute-start | bytes 98312 | tf_op jit(solution)/shard_map/ppermute | solution.py:22
  165.0 33.8 %copy-start.22 = (f32[8,16,64]{2,1,0:T(8,128)S(1)}, f32[8,16,64]{2,1,0:T(8,128)}, u32[]{:S(2)}) copy-start(f32[8,16,64]{2,1,0:T(8,128)} %pad_maximum_fusion.24) | copy-start | bytes 98308
  165.0 33.8 %copy-start.23 = (f32[8,16,64]{2,1,0:T(8,128)S(1)}, f32[8,16,64]{2,1,0:T(8,128)}, u32[]{:S(2)}) copy-start(f32[8,16,64]{2,1,0:T(8,128)} %get-tuple-element.18) | copy-start | bytes 98308
  165.0 33.8 %copy-start.24 = (f32[8,16,64]{2,1,0:T(8,128)S(1)}, f32[8,16,64]{2,1,0:T(8,128)}, u32[]{:S(2)}) copy-start(f32[8,16,64]{2,1,0:T(8,128)} %get-tuple-element.19) | copy-start | bytes 98308
  165.0 33.8 %copy-start.25 = (f32[8,16,64]{2,1,0:T(8,128)S(1)}, f32[8,16,64]{2,1,0:T(8,128)}, u32[]{:S(2)}) copy-start(f32[8,16,64]{2,1,0:T(8,128)} %get-tuple-element.97) | copy-start | bytes 98308
  165.0 33.8 %copy-start.26 = (f32[8,16,64]{2,1,0:T(8,128)S(1)}, f32[8,16,64]{2,1,0:T(8,128)}, u32[]{:S(2)}) copy-start(f32[8,16,64]{2,1,0:T(8,128)} %get-tuple-element.98) | copy-start | bytes 98308
  165.0 33.8 %copy-start.27 = (f32[8,16,64]{2,1,0:T(8,128)S(1)}, f32[8,16,64]{2,1,0:T(8,128)}, u32[]{:S(2)}) copy-start(f32[8,16,64]{2,1,0:T(8,128)} %get-tuple-element.99) | copy-start | bytes 98308
  165.0 33.8 %copy-start.35 = (f32[8,16,64]{2,1,0:T(8,128)S(1)}, f32[8,16,64]{2,1,0:T(8,128)}, u32[]{:S(2)}) copy-start(f32[8,16,64]{2,1,0:T(8,128)} %copy-done.34) | copy-start | bytes 98308
  211.8 3.7 %collective-permute-start.12 = (f32[2,1,32,128]{3,2,1,0:T(8,128)S(1)}, f32[2,1,32,128]{3,2,1,0:T(8,128)S(1)}, u32[]{:S(2)}, u32[]{:S(2)}) collective-permute-start(f32[2,1,32,128]{3,2,1,0:T(8,128)S(1)} %get-tuple-element.95), channel_id=1, source_target_pairs={{0,2},{2,4},{4,6},{6,8},{8,10},{10,12},{12,14},{1,3},{3,5},{5,7},{... | collective-permute-start | bytes 98312 | tf_op jit(solution)/shard_map/ppermute | solution.py:21
  213.2 5.8 %collective-permute-start.13 = (f32[2,1,32,128]{3,2,1,0:T(8,128)S(1)}, f32[2,1,32,128]{3,2,1,0:T(8,128)S(1)}, u32[]{:S(2)}, u32[]{:S(2)}) collective-permute-start(f32[2,1,32,128]{3,2,1,0:T(8,128)S(1)} %get-tuple-element.96), channel_id=1, source_target_pairs={{2,0},{4,2},{6,4},{8,6},{10,8},{12,10},{14,12},{3,1},{5,3},{7,5},{... | collective-permute-start | bytes 98312 | tf_op jit(solution)/shard_map/ppermute | solution.py:22
  219.2 5.1 %collective-permute-start.14 = (f32[2,1,32,128]{3,2,1,0:T(8,128)S(1)}, f32[2,1,32,128]{3,2,1,0:T(8,128)S(1)}, u32[]{:S(2)}, u32[]{:S(2)}) collective-permute-start(f32[2,1,32,128]{3,2,1,0:T(8,128)S(1)} %get-tuple-element.89), channel_id=1, source_target_pairs={{0,2},{2,4},{4,6},{6,8},{8,10},{10,12},{12,14},{1,3},{3,5},{5,7},{... | collective-permute-start | bytes 98312 | tf_op jit(solution)/shard_map/ppermute | solution.py:21
  222.7 5.8 %collective-permute-start.15 = (f32[2,1,32,128]{3,2,1,0:T(8,128)S(1)}, f32[2,1,32,128]{3,2,1,0:T(8,128)S(1)}, u32[]{:S(2)}, u32[]{:S(2)}) collective-permute-start(f32[2,1,32,128]{3,2,1,0:T(8,128)S(1)} %get-tuple-element.90), channel_id=1, source_target_pairs={{2,0},{4,2},{6,4},{8,6},{10,8},{12,10},{14,12},{3,1},{5,3},{7,5},{... | collective-permute-start | bytes 98312 | tf_op jit(solution)/shard_map/ppermute | solution.py:22
  229.9 5.5 %collective-permute-start.16 = (f32[2,1,64,256]{3,2,1,0:T(8,128)S(1)}, f32[2,1,64,256]{3,2,1,0:T(8,128)S(1)}, u32[]{:S(2)}, u32[]{:S(2)}) collective-permute-start(f32[2,1,64,256]{3,2,1,0:T(8,128)S(1)} %get-tuple-element.44), channel_id=1, source_target_pairs={{0,2},{2,4},{4,6},{6,8},{8,10},{10,12},{12,14},{1,3},{3,5},{5,7},{... | collective-permute-start | bytes 393224 | tf_op jit(solution)/shard_map/ppermute | solution.py:21
  232.9 6.9 %collective-permute-start.17 = (f32[2,1,64,256]{3,2,1,0:T(8,128)S(1)}, f32[2,1,64,256]{3,2,1,0:T(8,128)S(1)}, u32[]{:S(2)}, u32[]{:S(2)}) collective-permute-start(f32[2,1,64,256]{3,2,1,0:T(8,128)S(1)} %get-tuple-element.45), channel_id=1, source_target_pairs={{2,0},{4,2},{6,4},{8,6},{10,8},{12,10},{14,12},{3,1},{5,3},{7,5},{... | collective-permute-start | bytes 393224 | tf_op jit(solution)/shard_map/ppermute | solution.py:22
  240.5 6.2 %collective-permute-start.18 = (f32[2,1,64,256]{3,2,1,0:T(8,128)S(1)}, f32[2,1,64,256]{3,2,1,0:T(8,128)S(1)}, u32[]{:S(2)}, u32[]{:S(2)}) collective-permute-start(f32[2,1,64,256]{3,2,1,0:T(8,128)S(1)} %get-tuple-element.38), channel_id=1, source_target_pairs={{0,2},{2,4},{4,6},{6,8},{8,10},{10,12},{12,14},{1,3},{3,5},{5,7},{... | collective-permute-start | bytes 393224 | tf_op jit(solution)/shard_map/ppermute | solution.py:21
  244.3 6.9 %collective-permute-start.19 = (f32[2,1,64,256]{3,2,1,0:T(8,128)S(1)}, f32[2,1,64,256]{3,2,1,0:T(8,128)S(1)}, u32[]{:S(2)}, u32[]{:S(2)}) collective-permute-start(f32[2,1,64,256]{3,2,1,0:T(8,128)S(1)} %get-tuple-element.39), channel_id=1, source_target_pairs={{2,0},{4,2},{6,4},{8,6},{10,8},{12,10},{14,12},{3,1},{5,3},{7,5},{... | collective-permute-start | bytes 393224 | tf_op jit(solution)/shard_map/ppermute | solution.py:22
  252.2 7.0 %collective-permute-start.20 = (f32[2,1,64,256]{3,2,1,0:T(8,128)S(1)}, f32[2,1,64,256]{3,2,1,0:T(8,128)S(1)}, u32[]{:S(2)}, u32[]{:S(2)}) collective-permute-start(f32[2,1,64,256]{3,2,1,0:T(8,128)S(1)} %get-tuple-element.30), channel_id=1, source_target_pairs={{0,2},{2,4},{4,6},{6,8},{8,10},{10,12},{12,14},{1,3},{3,5},{5,7},{... | collective-permute-start | bytes 393224 | tf_op jit(solution)/shard_map/ppermute | solution.py:21
  256.7 6.9 %collective-permute-start.21 = (f32[2,1,64,256]{3,2,1,0:T(8,128)S(1)}, f32[2,1,64,256]{3,2,1,0:T(8,128)S(1)}, u32[]{:S(2)}, u32[]{:S(2)}) collective-permute-start(f32[2,1,64,256]{3,2,1,0:T(8,128)S(1)} %get-tuple-element.31), channel_id=1, source_target_pairs={{2,0},{4,2},{6,4},{8,6},{10,8},{12,10},{14,12},{3,1},{5,3},{7,5},{... | collective-permute-start | bytes 393224 | tf_op jit(solution)/shard_map/ppermute | solution.py:22
  (62 other events, 363.6 us)
where the time goes:
time: 271 us; the launch traced here: 269 us
  blocking collectives  66.4 us (25%)
  local copies, waits for them, and re-layouts  58.2 us (21%)
  starting transfers between devices  53.6 us (20%)
  waiting for transfers between devices  45.2 us (17%)
  other arithmetic  41.2 us (15%)
  between operations  4.72 us (2%)
    reshape x4, local copies, waits for them, and re-layouts, restrict_all(): values.reshape(leading + (width_x // 2, 2, width_y // 2, 2, width_z // 2,...  42.9 us
    ppermute x11, starting transfers between devices, with_halo(): before = lax.ppermute(last, axis, up)  39.4 us
    ppermute x11, waiting for transfers between devices, with_halo(): after = lax.ppermute(initial, axis, down)  38.5 us
    all_gather x1, blocking collectives, body(): coarse_logk = lax.all_gather(local_logk[2], 'slab', axis=0, tiled=True)  32.6 us
    all_gather x1, blocking collectives, spread_coarse(): whole_source = lax.all_gather(coarse_source, 'slab', axis=1, tiled=True)  30.7 us
    reduce_sum x10, other arithmetic, restrict_all(): return jnp.sum(blocks, axis=(offset + 1, offset + 3, offset + 5)) * 0.125  17.4 us
    ppermute x11, starting transfers between devices, with_halo(): after = lax.ppermute(initial, axis, down)  14.2 us
    ppermute x11, waiting for transfers between devices, with_halo(): before = lax.ppermute(last, axis, up)  6.62 us
  transfers between devices with their start and end apart: 22, of which 18 were waited for; matrix products, arithmetic and copies ran while one was open for 8% of the time, Pallas kernels for 0%

commit v1 on v0

v1 whole, which is shorter than its diff:
```python
import functools

import jax
import jax.numpy as jnp
from jax import lax
from jax.experimental import pallas as pl
from jax.experimental.pallas import tpu as pltpu
from jax.sharding import PartitionSpec as P

LEVELS = 5
SWEEPS = 2
COARSE_SWEEPS = 8
OMEGA = 0.8
REACH = 3

F32 = jnp.float32


def iota(shape, axis):
    return lax.broadcasted_iota(jnp.int32, shape, axis)


def pairing(rows, cols, row_shift, col_shift, dtype):
    shape = (rows, cols)
    same = jnp.right_shift(iota(shape, 0), row_shift) == jnp.right_shift(iota(shape, 1), col_shift)
    return jnp.where(same, 1.0, 0.0).astype(dtype)


def split(x, terms):
    parts = []
    for _ in range(terms):
        part = x.astype(jnp.bfloat16)
        parts.append(part)
        x = x - part.astype(F32)
    return parts


def right_mul(x, cols, row_shift, col_shift, terms):
    m = pairing(x.shape[1], cols, row_shift, col_shift, jnp.bfloat16)
    out = None
    for part in split(x, terms):
        y = jnp.dot(part, m, preferred_element_type=F32)
        out = y if out is None else out + y
    return out


def left_mul(x, rows, row_shift, col_shift, terms):
    if x.shape[0] < 16 or rows < 16:
        m = pairing(rows, x.shape[0], row_shift, col_shift, F32)
        return jnp.dot(m, x, precision=lax.Precision.HIGHEST, preferred_element_type=F32)
    m = pairing(rows, x.shape[0], row_shift, col_shift, jnp.bfloat16)
    out = None
    for part in split(x, terms):
        y = jnp.dot(m, part, preferred_element_type=F32)
        out = y if out is None else out + y
    return out


def restrict2(x, shape, terms=2):
    return left_mul(right_mul(x, shape[1], 1, 0, terms), shape[0], 0, 1, terms)


def prolong2(x, shape, terms=2):
    return right_mul(left_mul(x, shape[0], 1, 0, terms), shape[1], 0, 1, terms)


def roll(x, shift, axis):
    return pltpu.roll(x, shift % x.shape[axis], axis)


def nsum(x, size):
    iy, iz = iota(x.shape, 0), iota(x.shape, 1)
    total = jnp.where(iy > 0, roll(x, 1, 0), 0.0)
    total = total + jnp.where(iy < size[0] - 1, roll(x, -1, 0), 0.0)
    total = total + jnp.where(iz > 0, roll(x, 1, 1), 0.0)
    return total + jnp.where(iz < size[1] - 1, roll(x, -1, 1), 0.0)


def each(start, stop, fn):
    def step(p, carry):
        fn(p)
        return carry

    if isinstance(start, int) and isinstance(stop, int) and stop - start <= 2:
        for p in range(start, stop):
            fn(p)
        return
    lax.fori_loop(start, stop, step, 0)


def both(fn):
    for f in range(2):
        fn(f)


def diag_plane(center, below, above, x_now, x_last, size):
    iy = iota(center.shape, 0)
    d = below + above + nsum(center, size)
    outside = jnp.where(iy == 0, 2.0, 0.0) + jnp.where(iy == size[0] - 1, 2.0, 0.0)
    ends = jnp.where(x_now == 0, 2.0, 0.0) + jnp.where(x_now == x_last, 2.0, 0.0)
    return d + (outside + ends) * center


def inside(shape, size, x_now, x_last):
    ok = (iota(shape, 0) < size[0]) & (iota(shape, 1) < size[1])
    return ok & ((x_now >= 0) & (x_now <= x_last))


def kernel(ns, sizes, pads, seed_ref, weight_ref, recharge_ref, cells_ref, rates_ref, sens_ref,
           head_ref, adj_ref, zone_ref,
           b0, e0, d0, q0, g0, c0, ua, ub, l0, ie0, pv0,
           b1, l1, e1, ie1, d1, q1, g1, c1, va, vb, pv1,
           l2, b2, *rest):
    coarse = [rest[8 * i: 8 * i + 8] for i in range(3)]
    own_zone, other_zone = rest[24:26]
    s_halo, r_halo, s_l1, r_l1, s_b1, r_b1, s_l2, r_l2, s_b2, r_b2, s_z, r_z = rest[26:]
    me = lax.axis_index("slab")
    node = lax.axis_index("node")
    size0, size1, size2 = sizes[:3]
    pad1, pad2 = pads[1], pads[2]
    cx = recharge_ref.shape[0]
    last0 = cx * ns - 1
    own1 = 2 * REACH
    last1 = 2 * ns - 1

    def remote(src, dst, send, recv, slab):
        return pltpu.make_async_remote_copy(
            src_ref=src, dst_ref=dst, send_sem=send, recv_sem=recv,
            device_id={"slab": slab}, device_id_type=pl.DeviceIdType.MESH)

    zero0 = jnp.zeros(size0, F32)
    zero1 = jnp.zeros(pad1, F32)

    @pl.when(me == 0)
    def _():
        each(0, cx, lambda p: both(lambda f: b0.__setitem__((f, p), zero0)))

    @pl.when(me == ns - 1)
    def _():
        each(2 * cx, 3 * cx, lambda p: both(lambda f: b0.__setitem__((f, p), zero0)))

    def clear1(p):
        l1[p] = zero1
        b1[0, p] = zero1
        b1[1, p] = zero1

    each(0, 2 * own1 + 2, clear1)

    barrier = pltpu.get_barrier_semaphore()

    def greet(k):
        peer = lax.rem(me + k, ns)
        pl.semaphore_signal(barrier, inc=1, device_id={"slab": peer},
                            device_id_type=pl.DeviceIdType.MESH)

    each(1, ns, greet)
    pl.semaphore_signal(barrier, inc=1, device_id={"node": 1 - node},
                        device_id_type=pl.DeviceIdType.MESH)

    place = iota(size0, 0) * size0[1] + iota(size0, 1)

    def sources(p):
        value = recharge_ref[p]
        here = place + p * (size0[0] * size0[1])
        for w in range(cells_ref.shape[0]):
            value = value + jnp.where(here == cells_ref[w], rates_ref[w], 0.0)
        b0[0, cx + p] = value
        b0[1, cx + p] = sens_ref[p]

    each(0, cx, sources)
    pl.semaphore_wait(barrier, ns)

    half = cx // 2
    halo = [(1, cx + half, half, 0), (-1, cx, 2 * cx, 1),
            (1, cx, 0, 2), (-1, cx + half, 2 * cx + half, 3)]

    def halo_copy(way, src, dst, i, slab):
        return remote(b0.at[:, pl.ds(src, half)], b0.at[:, pl.ds(dst, half)],
                      s_halo.at[i], r_halo.at[i], slab)

    def in_range(slab):
        return (slab >= 0) & (slab < ns)

    def halo_start(i):
        way = halo[i][0]

        @pl.when(in_range(me + way))
        def _():
            halo_copy(*halo[i], me + way).start()

    def halo_wait(i):
        way = halo[i][0]

        @pl.when(in_range(me - way))
        def _():
            halo_copy(*halo[i], me - way).wait_recv()

    for i in range(4):
        halo_start(i)

    def near_copy(ref, send, recv, lead, d, slab):
        src, dst = pl.ds(own1, 2), pl.ds(own1 - 2 * d, 2)
        index = (slice(None),) if lead else ()
        return remote(ref.at[index + (src,)], ref.at[index + (dst,)],
                      send.at[d + REACH], recv.at[d + REACH], slab)

    steps = [s * d for d in range(1, REACH + 1) for s in (1, -1)]

    def near_start(*args):
        for d in steps:
            @pl.when(in_range(me + d))
            def _():
                near_copy(*args, d, me + d).start()

    def near_wait(*args, distances):
        for d in steps:
            if abs(d) in distances:
                @pl.when(in_range(me - d))
                def _():
                    near_copy(*args, d, me - d).wait_recv()

    def near_sent(*args):
        for d in steps:
            @pl.when(in_range(me + d))
            def _():
                near_copy(*args, d, me + d).wait_send()

    def all_copy(ref, send, recv, lead, k, slab, owner):
        index = (slice(None),) if lead else ()
        at = ref.at[index + (pl.ds(owner, 1),)]
        return remote(at, at, send.at[k], recv.at[k], slab)

    def all_start(*args):
        each(1, ns, lambda k: all_copy(*args, k, lax.rem(me + k, ns), me).start())

    def all_wait(*args):
        def wait(k):
            peer = lax.rem(me - k + ns, ns)
            all_copy(*args, k, peer, peer).wait_recv()

        each(1, ns, wait)

    def all_sent(*args):
        each(1, ns, lambda k: all_copy(*args, k, lax.rem(me + k, ns), me).wait_send())

    seed_part = seed_ref[0] * 277803737 + 1013904223
    hashed_place = place * 747796405
    first0 = me * cx - cx

    def logk_plane(p):
        x_now = first0 - 1 + p
        q = hashed_place + (x_now * (size0[0] * size0[1]) * 747796405 + seed_part)
        q = jnp.bitwise_xor(q, lax.shift_right_logical(q, jnp.full(size0, 15, jnp.int32)))
        q = q * 1274126177
        q = jnp.bitwise_xor(q, lax.shift_right_logical(q, jnp.full(size0, 13, jnp.int32)))
        low = jnp.bitwise_and(q, 65535)
        logk = 3.0 * (low.astype(F32) / 65536.0) - 1.5
        l0[p] = logk
        known = (x_now >= 0) & (x_now <= last0)
        e0[p] = jnp.where(known, jnp.exp(0.5 * logk), 0.0)
        ie0[p] = jnp.exp(-0.5 * logk)

    each(0, 3 * cx + 2, logk_plane)
    for i in range(2):
        pair = l0[cx + 1 + 2 * i] + l0[cx + 2 + 2 * i]
        l1[own1 + i] = restrict2(pair, pad1, 3) * 0.125
    near_start(l1, s_l1, r_l1, False)
    l2[pl.ds(me, 1)] = (restrict2(l1[own1] + l1[own1 + 1], pad2, 3) * 0.125)[None]
    all_start(l2, s_l2, r_l2, False)

    def operator0(p):
        x_now = first0 + p
        center = e0[p + 1]
        d = diag_plane(center, e0[p], e0[p + 2], x_now, last0, size0)
        known = (x_now >= 0) & (x_now <= last0)
        q = jnp.where(known, OMEGA / d, 0.0)
        d0[p] = d
        q0[p] = q
        g0[p] = q * center

    each(0, 3 * cx, operator0)

    def first0_c(p):
        q = q0[p]
        c0[0, p] = q * b0[0, p]
        c0[1, p] = q * b0[1, p]

    def first_sweeps(u, c, g, size, p):
        gain = g[p]

        def one(f):
            now = c[f, p]
            total = c[f, p - 1] + c[f, p + 1] + nsum(now, size)
            u[f, p] = (2.0 - OMEGA) * now + gain * total

        both(one)

    def sweep(u, c, g, out, size, p, gp=None, cp=None):
        gp = p if gp is None else gp
        cp = p if cp is None else cp
        gain = g[gp]

        def one(f):
            now = u[f, p]
            total = u[f, p - 1] + u[f, p + 1] + nsum(now, size)
            out[f, p] = (1.0 - OMEGA) * now + c[f, cp] + gain * total

        both(one)

    def residue(u, b, e, d, size, f, p, ep, dp, bp):
        now = u[f, p]
        total = u[f, p - 1] + u[f, p + 1] + nsum(now, size)
        return b[f, bp] + e[ep] * total - d[dp] * now

    each(cx, 2 * cx, first0_c)

    near_wait(l1, s_l1, r_l1, False, distances=(1, 2, 3))
    first1 = 2 * me - own1
    width1 = 2 * own1 + 2

    def exp1(p):
        x_now = first1 + p
        ok = inside(pad1, size1, x_now, last1)
        logk = l1[p]
        e1[p] = jnp.where(ok, jnp.exp(0.5 * logk), 0.0)
        ie1[p] = jnp.where(ok, jnp.exp(-0.5 * logk), 0.0)

    each(0, width1, exp1)

    def operator1(p):
        x_now = first1 + p
        center = e1[p]
        d = diag_plane(center, e1[p - 1], e1[p + 1], x_now, last1, size1)
        q = jnp.where(inside(pad1, size1, x_now, last1), OMEGA / d, 0.0)
        d1[p] = d
        q1[p] = q
        g1[p] = q * center

    each(1, width1 - 1, operator1)

    halo_wait(0)
    halo_wait(1)
    each(half, cx, first0_c)
    each(2 * cx, 2 * cx + half, first0_c)
    each(cx - 1, 2 * cx + 1, functools.partial(first_sweeps, ua, c0, g0, size0))

    for f in range(2):
        for i in range(2):
            p = cx + 2 * i
            pair = (residue(ua, b0, e0, d0, size0, f, p, p + 1, p, p)
                    + residue(ua, b0, e0, d0, size0, f, p + 1, p + 2, p + 1, p + 1))
            b1[f, own1 + i] = restrict2(pair, pad1) * 0.5
    near_start(b1, s_b1, r_b1, True)

    all_wait(l2, s_l2, r_l2, False)
    counts = [ns >> i for i in range(3)]
    logs = l2
    for i in range(3):
        e, ie, d, q, g, c, u, w = coarse[i]
        size, pad, n = sizes[2 + i], pads[2 + i], counts[i]
        e[0] = jnp.zeros(pad, F32)
        e[n + 1] = jnp.zeros(pad, F32)
        for ref in (u, w):
            for f in range(2):
                ref[f, 0] = jnp.zeros(pad, F32)
                ref[f, n + 1] = jnp.zeros(pad, F32)
        source = l2 if i == 0 else None

        def exps(p, e=e, ie=ie, size=size, pad=pad, n=n, i=i, d=d):
            if i == 0:
                logk = l2[p]
            else:
                above = coarse[i - 1][4] if i > 1 else l2
                logk = restrict2(above[2 * p] + above[2 * p + 1], pad, 3) * 0.125
                g_now = coarse[i][4]
                g_now[p] = logk
            ok = inside(pad, size, p, n - 1)
            e[p + 1] = jnp.where(ok, jnp.exp(0.5 * logk), 0.0)
            ie[p] = jnp.where(ok, jnp.exp(-0.5 * logk), 0.0)

        each(0, n, exps)
    for i in range(3):
        e, ie, d, q, g, c, u, w = coarse[i]
        size, pad, n = sizes[2 + i], pads[2 + i], counts[i]

        def ops(p, e=e, d=d, q=q, g=g, size=size, pad=pad, n=n):
            center = e[p + 1]
            dd = diag_plane(center, e[p], e[p + 2], p, n - 1, size)
            qq = jnp.where(inside(pad, size, p, n - 1), OMEGA / dd, 0.0)
            d[p] = dd
            q[p] = qq
            g[p] = qq * center

        each(0, n, ops)

    def first1_c(p):
        q = q1[p]
        c1[0, p] = q * b1[0, p]
        c1[1, p] = q * b1[1, p]

    near_wait(b1, s_b1, r_b1, True, distances=(1,))
    each(own1 - 2, own1 + 4, first1_c)
    each(own1 - 1, own1 + 3, functools.partial(first_sweeps, va, c1, g1, size1))
    for f in range(2):
        pair = (residue(va, b1, e1, d1, size1, f, own1, own1, own1, own1)
                + residue(va, b1, e1, d1, size1, f, own1 + 1, own1 + 1, own1 + 1, own1 + 1))
        b2[f, pl.ds(me, 1)] = (restrict2(pair, pad2) * 0.5)[None]
    all_start(b2, s_b2, r_b2, True)

    halo_wait(2)
    halo_wait(3)
    each(0, half, first0_c)
    each(2 * cx + half, 3 * cx, first0_c)
    each(1, cx - 1, functools.partial(first_sweeps, ua, c0, g0, size0))
    each(2 * cx + 1, 3 * cx - 1, functools.partial(first_sweeps, ua, c0, g0, size0))
    near_wait(b1, s_b1, r_b1, True, distances=(2, 3))
    each(own1 - 5, own1 - 2, first1_c)
    each(own1 + 4, own1 + 7, first1_c)
    each(own1 - 4, own1 - 1, functools.partial(first_sweeps, va, c1, g1, size1))
    each(own1 + 3, own1 + 6, functools.partial(first_sweeps, va, c1, g1, size1))

    all_wait(b2, s_b2, r_b2, True)

    def solve(i, source):
        e, ie, d, q, g, c, u, w = coarse[i]
        size, pad, n = sizes[2 + i], pads[2 + i], counts[i]

        def begin(p):
            def one(f):
                value = q[p] * source[f, p]
                c[f, p] = value
                u[f, p + 1] = value

            both(one)

        each(0, n, begin)

        def full(src, dst):
            each(1, n + 1, lambda p: sweep(src, c, g, dst, size, p, p - 1, p - 1))

        if i == 2:
            now, then = u, w
            for _ in range(COARSE_SWEEPS - 1):
                full(now, then)
                now, then = then, now
            return now
        full(u, w)
        below = rest_source[i + 1]

        def down(p):
            def one(f):
                pair = (residue(w, source, e, d, size, f, 2 * p + 1, 2 * p + 1, 2 * p, 2 * p)
                        + residue(w, source, e, d, size, f, 2 * p + 2, 2 * p + 2, 2 * p + 1, 2 * p + 1))
                below[f, p] = restrict2(pair, pads[3 + i]) * 0.5

            both(one)

        each(0, counts[i + 1], down)
        fix = solve(i + 1, below)
        fix_inv = coarse[i + 1][1]

        def up(p):
            def one(f):
                add = prolong2(fix[f, p + 1] * fix_inv[p], pad)
                w[f, 2 * p + 1] = w[f, 2 * p + 1] + e[2 * p + 1] * add
                w[f, 2 * p + 2] = w[f, 2 * p + 2] + e[2 * p + 2] * add

            both(one)

        each(0, counts[i + 1], up)
        full(w, u)
        full(u, w)
        return w

    rest_source = [b2, coarse[1][6], coarse[2][6]]
    rest_source = [b2, pv0, pv1]
    top = solve(0, b2)
    top_inv = coarse[0][1]

    def correct1(k):
        at = jnp.clip(me - 2 + k, 0, ns - 1)
        p = own1 - 4 + 2 * k

        def one(f):
            add = prolong2(top[f, at + 1] * top_inv[at], pad1)
            va[f, p] = va[f, p] + e1[p] * add
            va[f, p + 1] = va[f, p + 1] + e1[p + 1] * add

        both(one)

    each(0, 5, correct1)
    each(own1 - 3, own1 + 5, functools.partial(sweep, va, c1, g1, vb, size1))
    each(own1 - 2, own1 + 4, functools.partial(sweep, vb, c1, g1, va, size1))

    def correct0(f, l, planes):
        add = prolong2(va[f, l] * ie1[l], size0)
        for p in planes:
            ua[f, p] = ua[f, p] + e0[p + 1] * add

    for f in range(2):
        correct0(f, own1 - 2, (1,))
        correct0(f, own1 + 3, (3 * cx - 2,))

    def middle(k):
        p = 2 + 2 * k
        both(lambda f: correct0(f, own1 - 1 + k, (p, p + 1)))

    each(0, 4, middle)
    each(2, 3 * cx - 2, functools.partial(sweep, ua, c0, g0, ub, size0))
    each(3, 3 * cx - 3, functools.partial(sweep, ub, c0, g0, ua, size0))

    def heads(p):
        inv = ie0[p + 1]
        ub[0, p] = ua[0, p] * inv
        ub[1, p] = ua[1, p] * inv

    each(cx - 1, 2 * cx + 1, heads)

    iy, iz = iota(size0, 0), iota(size0, 1)
    y_end = (iy == 0) | (iy == size0[0] - 1)

    def gradient(p, carry):
        plain, by_y, by_z = carry
        h, a, e = ub[0, p], ub[1, p], e0[p + 1]
        head_ref[0, p - cx] = h
        adj_ref[0, p - cx] = a
        lower = e * e0[p] * (h - ub[0, p - 1]) * (a - ub[1, p - 1])
        upper = e * e0[p + 2] * (h - ub[0, p + 1]) * (a - ub[1, p + 1])
        x_now = first0 + p
        edge = 2.0 * ua[0, p] * ua[1, p]
        ends = jnp.where(x_now == 0, 1.0, 0.0) + jnp.where(x_now == last0, 1.0, 0.0)
        plain = plain + 0.5 * (lower + upper) + edge * (ends + jnp.where(y_end, 1.0, 0.0))
        by_y = by_y + e * roll(e, 1, 0) * (h - roll(h, 1, 0)) * (a - roll(a, 1, 0))
        by_z = by_z + e * roll(e, 1, 1) * (h - roll(h, 1, 1)) * (a - roll(a, 1, 1))
        return plain, by_y, by_z

    plain, by_y, by_z = lax.fori_loop(cx, 2 * cx, gradient, (zero0, zero0, zero0))
    by_y = jnp.where(iy > 0, by_y, 0.0)
    by_z = jnp.where(iz > 0, by_z, 0.0)
    cells = plain + 0.5 * (by_y + roll(by_y, -1, 0) + by_z + roll(by_z, -1, 1))
    zy, zz = zone_ref.shape[1:]
    zone = right_mul(left_mul(cells, zy, 0, 2, 3), zz, 2, 0, 3)
    weight_sum = weight_ref[0]
    for w in range(1, weight_ref.shape[0]):
        weight_sum = weight_sum + weight_ref[w]
    own = jnp.full(zone.shape, weight_ref[node], jnp.int32).astype(F32)
    portion = own / jnp.full(zone.shape, weight_sum, jnp.int32).astype(F32)
    own_zone[...] = -(portion * zone)
    zone_copy = pltpu.make_async_remote_copy(
        src_ref=own_zone, dst_ref=other_zone, send_sem=s_z, recv_sem=r_z,
        device_id={"node": 1 - node}, device_id_type=pl.DeviceIdType.MESH)
    zone_copy.start()

    for i in range(4):
        way = halo[i][0]

        @pl.when(in_range(me + way))
        def _():
            halo_copy(*halo[i], me + way).wait_send()

    near_sent(l1, s_l1, r_l1, False)
    near_sent(b1, s_b1, r_b1, True)
    all_sent(l2, s_l2, r_l2, False)
    all_sent(b2, s_b2, r_b2, True)
    zone_copy.wait()
    zone_ref[0] = own_zone[...] + other_zone[...]


def body(ns, field_seeds, quad_weight, recharge, well_cells, well_rates, sensitivity):
    cx, ny, nz = recharge.shape
    sizes = [(ny >> l, nz >> l) for l in range(LEVELS)]
    pads = [(max(y, 8), max(z, 128)) for y, z in sizes]
    wide = 3 * cx
    near = 4 * REACH + 2
    vmem, smem = pltpu.VMEM, pltpu.SMEM
    p0, p1, p2 = pads[:3]
    dma = pltpu.SemaphoreType.DMA
    scratch = [
        vmem((2, wide) + p0, F32), vmem((wide + 2,) + p0, F32), vmem((wide,) + p0, F32),
        vmem((wide,) + p0, F32), vmem((wide,) + p0, F32), vmem((2, wide) + p0, F32),
        vmem((2, wide) + p0, F32), vmem((2, wide) + p0, F32), vmem((wide + 2,) + p0, F32),
        vmem((wide + 2,) + p0, F32), vmem((2, ns // 2) + pads[3], F32),
        vmem((2, near) + p1, F32), vmem((near,) + p1, F32), vmem((near,) + p1, F32),
        vmem((near,) + p1, F32), vmem((near,) + p1, F32), vmem((near,) + p1, F32),
        vmem((near,) + p1, F32), vmem((2, near) + p1, F32), vmem((2, near) + p1, F32),
        vmem((2, near) + p1, F32), vmem((2, ns // 4) + pads[4], F32),
        vmem((ns,) + p2, F32), vmem((2, ns) + p2, F32),
    ]
    for i in range(3):
        n, pad = ns >> i, pads[2 + i]
        scratch += [vmem((n + 2,) + pad, F32), vmem((n,) + pad, F32), vmem((n,) + pad, F32),
                    vmem((n,) + pad, F32), vmem((n,) + pad, F32), vmem((2, n) + pad, F32),
                    vmem((2, n + 2) + pad, F32), vmem((2, n + 2) + pad, F32)]
    zone = (ny // 4, nz // 4)
    scratch += [vmem(zone, F32), vmem(zone, F32)]
    spread = 2 * REACH + 1
    scratch += [dma((4,)), dma((4,)), dma((spread,)), dma((spread,)), dma((spread,)), dma((spread,)),
                dma((ns,)), dma((ns,)), dma((ns,)), dma((ns,)), dma, dma]
    in_v, in_s = pl.BlockSpec(memory_space=vmem), pl.BlockSpec(memory_space=smem)
    field = jax.ShapeDtypeStruct((1, cx, ny, nz), F32)
    return pl.pallas_call(
        functools.partial(kernel, ns, sizes, pads),
        out_shape=(field, field, jax.ShapeDtypeStruct((1,) + zone, F32)),
        in_specs=[in_s, in_s, in_v, in_s, in_s, in_v],
        out_specs=(in_v, in_v, in_v),
        scratch_shapes=scratch,
        compiler_params=pltpu.CompilerParams(
            collective_id=0, has_side_effects=True, vmem_limit_bytes=48 * 1024 * 1024),
    )(field_seeds, quad_weight, recharge, well_cells, well_rates, sensitivity)


def solution(mesh):
    placed = (
        P(("groups", "node")),
        P("groups"),
        P(("groups", "slab"), None, None),
        P(("groups", "slab")),
        P(("groups", "slab")),
        P(("groups", "slab"), None, None),
    )
    return jax.shard_map(
        functools.partial(body, mesh.shape["slab"]),
        mesh=mesh,
        in_specs=placed,
        out_specs=(
            P(("groups", "node"), "slab", None, None),
            P(("groups", "node"), "slab", None, None),
            P(("groups", "slab"), None, None),
        ),
        check_vma=False,
    )
```

time: 271 us -> 70.7 us (0.26)
  blocking collectives: 66.4 us -> 0 us
  Pallas kernels: 0 us -> 65.3 us
  local copies, waits for them, and re-layouts: 58.2 us -> 3.91 us
  starting transfers between devices: 53.6 us -> 0 us
  waiting for transfers between devices: 45.2 us -> 0 us
  other arithmetic: 41.2 us -> 0 us
  between operations: 4.72 us -> 1.37 us
    pallas_call x0 -> x1, Pallas kernels: none -> 65.3 us  [body(): pl.pallas_call(functools.partial(kernel, ns, sizes, pads), out_shape=(fie...]
    all_gather x2 -> x0, blocking collectives: 63.3 us -> none  [the longest x1 32.6 us: body(): coarse_logk = lax.all_gather(local_logk[2], 'slab', axis=0, tiled=True)]
    ppermute x22 -> x0, starting transfers between devices: 53.6 us -> none  [the longest x11 39.4 us: with_halo(): before = lax.ppermute(last, axis, up)]
    ppermute x22 -> x0, waiting for transfers between devices: 45.2 us -> none  [the longest x11 38.5 us: with_halo(): after = lax.ppermute(initial, axis, down)]
    reshape x11 -> x0, local copies, waits for them, and re-layouts: 44 us -> none  [the longest x4 42.9 us: restrict_all(): values.reshape(leading + (width_x // 2, 2, width_y // 2, 2, width_z // 2,...]
    reduce_sum x13 -> x0, other arithmetic: 19.1 us -> none  [the longest x10 17.4 us: restrict_all(): return jnp.sum(blocks, axis=(offset + 1, offset + 3, offset + 5)) * 0.125]
    add x27 -> x0, other arithmetic: 6.14 us -> none  [the longest x18 4.26 us: vcycle(): iterate + inverse * (source - apply_operator(operator_set, pad_fn(iterate)))]
    reduce_sum x4 -> x0, local copies, waits for them, and re-layouts: 6.06 us -> none  [the longest x3 3.91 us: restrict_all(): return jnp.sum(blocks, axis=(offset + 1, offset + 3, offset + 5)) * 0.125]
  transfers between devices with their start and end apart: 22 -> 0, of which waited for: 18 -> 0; matrix products, arithmetic and copies ran while one was open for 8% -> 0% of each run, Pallas kernels for 0% -> 0%
where the time goes in v1:
time: 70.7 us; the launch traced here: 70.5 us
  Pallas kernels  65.3 us (92%)
  local copies, waits for them, and re-layouts  3.91 us (6%)
  between operations  1.37 us (2%)
    pallas_call x1, Pallas kernels, body(): pl.pallas_call(functools.partial(kernel, ns, sizes, pads), out_shape=(fie...  65.3 us
    unnamed x13, local copies, waits for them, and re-layouts  3.91 us

profile of v1, /device:TPU:0, one launch (start us, length us, event | category | flops | bytes accessed | tf_op | source)
XLA Modules:
  0.0 70.5 jit_solution(6964598629893644816)
XLA Ops:
  0.6 0.0 copy-start.4
  0.6 0.0 copy-start.3
  0.7 0.0 copy-start.2
  1.3 0.0 copy-done.4
  1.3 0.0 copy-done.3
  1.4 0.0 copy-done.2
  1.4 0.0 copy-start
  1.4 0.9 %copy-done = f32[4,64,256]{2,1,0:T(8,128)S(1)} copy-done((f32[4,64,256]{2,1,0:T(8,128)S(1)}, f32[4,64,256]{2,1,0:T(8,128)}, u32[]{:S(2)}) %copy-start) | copy-done | bytes 262168
  2.3 0.0 copy-start.1
  2.3 0.9 %copy-done.1 = f32[4,64,256]{2,1,0:T(8,128)S(1)} copy-done((f32[4,64,256]{2,1,0:T(8,128)S(1)}, f32[4,64,256]{2,1,0:T(8,128)}, u32[]{:S(2)}) %copy-start.1) | copy-done | bytes 262168
  3.3 65.3 %shard_map.85 = (f32[1,4,64,256]{3,2,1,0:T(8,128)S(1)}, f32[1,4,64,256]{3,2,1,0:T(8,128)S(1)}, f32[1,16,64]{2,1,0:T(8,128)S(1)}) custom-call(s32[1]{0:T(128)S(6)} %copy.12.seed_ref, s32[2]{0:T(128)S(1)} %copy-done.2, f32[4,64,256]{2,1,0:T(8,128)S(1)} %copy-done, s32[8]{0:T(128)S(1)} %copy-done.3, f32[8]{0:T(128)S(1)} %copy-done.4, f32[4,64,256]{2,1,0:T(8,128)S(1)} %copy-done.1), custom_call_target="tpu_custom_call" | custom-call | tf_op jit(solution)/shard_map/pallas_call | solution.py:601
  68.5 0.7 copy.13
  69.2 0.7 copy.14
  69.9 0.6 copy.15
Async XLA Ops:
  0.6 0.7 copy-start.4
  0.6 0.7 copy-start.3
  0.7 0.7 copy-start.2
  1.4 1.0 %copy-start = (f32[4,64,256]{2,1,0:T(8,128)S(1)}, f32[4,64,256]{2,1,0:T(8,128)}, u32[]{:S(2)}) copy-start(f32[4,64,256]{2,1,0:T(8,128)} %recharge_ref.1) | copy-start | bytes 786436
  2.3 0.9 %copy-start.1 = (f32[4,64,256]{2,1,0:T(8,128)S(1)}, f32[4,64,256]{2,1,0:T(8,128)}, u32[]{:S(2)}) copy-start(f32[4,64,256]{2,1,0:T(8,128)} %sens_ref.1) | copy-start | bytes 786436

commit v2 on v1

--- a/solution.py
+++ b/solution.py
@@ -20,10 +20,21 @@
     return lax.broadcasted_iota(jnp.int32, shape, axis)
 
 
-def pairing(rows, cols, row_shift, col_shift, dtype):
+def matrix(rows, cols, rule, dtype=jnp.bfloat16):
     shape = (rows, cols)
-    same = jnp.right_shift(iota(shape, 0), row_shift) == jnp.right_shift(iota(shape, 1), col_shift)
-    return jnp.where(same, 1.0, 0.0).astype(dtype)
+    return jnp.where(rule(iota(shape, 0), iota(shape, 1)), 1.0, 0.0).astype(dtype)
+
+
+def half_of(i):
+    return jnp.right_shift(i, 1)
+
+
+def coarsen(i, j):
+    return half_of(i) == j
+
+
+def refine(i, j):
+    return i == half_of(j)
 
 
 def split(x, terms):
@@ -35,8 +46,8 @@
     return parts
 
 
-def right_mul(x, cols, row_shift, col_shift, terms):
-    m = pairing(x.shape[1], cols, row_shift, col_shift, jnp.bfloat16)
+def right_mul(x, cols, rule, terms=2):
+    m = matrix(x.shape[1], cols, rule)
     out = None
     for part in split(x, terms):
         y = jnp.dot(part, m, preferred_element_type=F32)
@@ -44,11 +55,8 @@
     return out
 
 
-def left_mul(x, rows, row_shift, col_shift, terms):
-    if x.shape[0] < 16 or rows < 16:
-        m = pairing(rows, x.shape[0], row_shift, col_shift, F32)
-        return jnp.dot(m, x, precision=lax.Precision.HIGHEST, preferred_element_type=F32)
-    m = pairing(rows, x.shape[0], row_shift, col_shift, jnp.bfloat16)
+def left_mul(x, rows, rule, terms=2):
+    m = matrix(rows, x.shape[0], lambda i, j: rule(j, i))
     out = None
     for part in split(x, terms):
         y = jnp.dot(m, part, preferred_element_type=F32)
@@ -57,31 +65,33 @@
 
 
 def restrict2(x, shape, terms=2):
-    return left_mul(right_mul(x, shape[1], 1, 0, terms), shape[0], 0, 1, terms)
+    return left_mul(right_mul(x, shape[1], coarsen, terms), shape[0], coarsen, terms)
 
 
 def prolong2(x, shape, terms=2):
-    return right_mul(left_mul(x, shape[0], 1, 0, terms), shape[1], 0, 1, terms)
+    return right_mul(left_mul(x, shape[0], refine, terms), shape[1], refine, terms)
 
 
 def roll(x, shift, axis):
     return pltpu.roll(x, shift % x.shape[axis], axis)
 
 
-def nsum(x, size):
+def nsum(x, size, fields=1):
     iy, iz = iota(x.shape, 0), iota(x.shape, 1)
+    if fields > 1:
+        iz = jnp.bitwise_and(iz, size[1] - 1)
     total = jnp.where(iy > 0, roll(x, 1, 0), 0.0)
     total = total + jnp.where(iy < size[0] - 1, roll(x, -1, 0), 0.0)
     total = total + jnp.where(iz > 0, roll(x, 1, 1), 0.0)
     return total + jnp.where(iz < size[1] - 1, roll(x, -1, 1), 0.0)
 
 
-def each(start, stop, fn):
+def each(start, stop, fn, unroll=2):
     def step(p, carry):
         fn(p)
         return carry
 
-    if isinstance(start, int) and isinstance(stop, int) and stop - start <= 2:
+    if stop - start <= unroll:
         for p in range(start, stop):
             fn(p)
         return
@@ -93,27 +103,27 @@
         fn(f)
 
 
-def diag_plane(center, below, above, x_now, x_last, size):
+def diag_plane(center, below, above, x_now, x_last, size, fields=1):
     iy = iota(center.shape, 0)
-    d = below + above + nsum(center, size)
+    d = below + above + nsum(center, size, fields)
     outside = jnp.where(iy == 0, 2.0, 0.0) + jnp.where(iy == size[0] - 1, 2.0, 0.0)
     ends = jnp.where(x_now == 0, 2.0, 0.0) + jnp.where(x_now == x_last, 2.0, 0.0)
     return d + (outside + ends) * center
 
 
-def inside(shape, size, x_now, x_last):
-    ok = (iota(shape, 0) < size[0]) & (iota(shape, 1) < size[1])
+def inside(shape, size, x_now, x_last, fields=1):
+    ok = (iota(shape, 0) < size[0]) & (iota(shape, 1) < fields * size[1])
     return ok & ((x_now >= 0) & (x_now <= x_last))
 
 
 def kernel(ns, sizes, pads, seed_ref, weight_ref, recharge_ref, cells_ref, rates_ref, sens_ref,
            head_ref, adj_ref, zone_ref,
-           b0, e0, d0, q0, g0, c0, ua, ub, l0, ie0, pv0,
-           b1, l1, e1, ie1, d1, q1, g1, c1, va, vb, pv1,
+           b0, e0, d0, q0, g0, c0, ua, ub, l0, ie0, b3,
+           b1, l1, e1, ie1, d1, q1, g1, c1, va, vb, b4,
            l2, b2, *rest):
     coarse = [rest[8 * i: 8 * i + 8] for i in range(3)]
     own_zone, other_zone = rest[24:26]
-    s_halo, r_halo, s_l1, r_l1, s_b1, r_b1, s_l2, r_l2, s_b2, r_b2, s_z, r_z = rest[26:]
+    s_halo, r_halo, s_in, s_l1, r_l1, s_b1, r_b1, s_l2, r_l2, s_b2, r_b2, s_z, r_z = rest[26:]
     me = lax.axis_index("slab")
     node = lax.axis_index("node")
     size0, size1, size2 = sizes[:3]
@@ -157,16 +167,22 @@
     pl.semaphore_signal(barrier, inc=1, device_id={"node": 1 - node},
                         device_id_type=pl.DeviceIdType.MESH)
 
+    loads = [pltpu.make_async_copy(ref, b0.at[f, pl.ds(cx, cx)], s_in.at[f])
+             for f, ref in enumerate((recharge_ref, sens_ref))]
+    for load in loads:
+        load.start()
+
     place = iota(size0, 0) * size0[1] + iota(size0, 1)
 
     def sources(p):
-        value = recharge_ref[p]
+        value = b0[0, cx + p]
         here = place + p * (size0[0] * size0[1])
         for w in range(cells_ref.shape[0]):
             value = value + jnp.where(here == cells_ref[w], rates_ref[w], 0.0)
         b0[0, cx + p] = value
-        b0[1, cx + p] = sens_ref[p]
-
+
+    for load in loads:
+        load.wait()
     each(0, cx, sources)
     pl.semaphore_wait(barrier, ns)
 
@@ -175,8 +191,15 @@
             (1, cx, 0, 2), (-1, cx + half, 2 * cx + half, 3)]
 
     def halo_copy(way, src, dst, i, slab):
-        return remote(b0.at[:, pl.ds(src, half)], b0.at[:, pl.ds(dst, half)],
+        field = pl.ds(node, 1)
+        return remote(b0.at[field, pl.ds(src, half)], b0.at[field, pl.ds(dst, half)],
                       s_halo.at[i], r_halo.at[i], slab)
+
+    def pass_copy(way, src, dst, i, slab, field):
+        at = b0.at[pl.ds(field, 1), pl.ds(dst, half)]
+        return pltpu.make_async_remote_copy(
+            src_ref=at, dst_ref=at, send_sem=s_halo.at[4 + i], recv_sem=r_halo.at[4 + i],
+            device_id={"node": 1 - node}, device_id_type=pl.DeviceIdType.MESH)
 
     def in_range(slab):
         return (slab >= 0) & (slab < ns)
@@ -188,14 +211,33 @@
         def _():
             halo_copy(*halo[i], me + way).start()
 
-    def halo_wait(i):
+    def halo_pass(i):
         way = halo[i][0]
 
         @pl.when(in_range(me - way))
         def _():
             halo_copy(*halo[i], me - way).wait_recv()
-
-    for i in range(4):
+            pass_copy(*halo[i], me, node).start()
+
+    def halo_wait(i):
+        way = halo[i][0]
+
+        @pl.when(in_range(me - way))
+        def _():
+            pass_copy(*halo[i], me, 1 - node).wait_recv()
+
+    def halo_sent(i):
+        way = halo[i][0]
+
+        @pl.when(in_range(me + way))
+        def _():
+            halo_copy(*halo[i], me + way).wait_send()
+
+        @pl.when(in_range(me - way))
+        def _():
+            pass_copy(*halo[i], me, node).wait_send()
+
+    for i in range(2):
         halo_start(i)
 
     def near_copy(ref, send, recv, lead, d, slab):
@@ -265,7 +307,9 @@
         pair = l0[cx + 1 + 2 * i] + l0[cx + 2 + 2 * i]
         l1[own1 + i] = restrict2(pair, pad1, 3) * 0.125
     near_start(l1, s_l1, r_l1, False)
-    l2[pl.ds(me, 1)] = (restrict2(l1[own1] + l1[own1 + 1], pad2, 3) * 0.125)[None]
+    both_fields = right_mul(l1[own1] + l1[own1 + 1], pad2[1],
+                            lambda i, j: half_of(i) == jnp.bitwise_and(j, size2[1] - 1), 3)
+    l2[pl.ds(me, 1)] = (left_mul(both_fields, pad2[0], coarsen, 3) * 0.125)[None]
     all_start(l2, s_l2, r_l2, False)
 
     def operator0(p):
@@ -314,6 +358,22 @@
 
     each(cx, 2 * cx, first0_c)
 
+    halo_pass(0)
+    halo_pass(1)
+    halo_wait(0)
+    halo_wait(1)
+    each(half, cx, first0_c)
+    each(2 * cx, 2 * cx + half, first0_c)
+    each(cx - 1, 2 * cx + 1, functools.partial(first_sweeps, ua, c0, g0, size0))
+
+    for f in range(2):
+        for i in range(2):
+            p = cx + 2 * i
+            pair = (residue(ua, b0, e0, d0, size0, f, p, p + 1, p, p)
+                    + residue(ua, b0, e0, d0, size0, f, p + 1, p + 2, p + 1, p + 1))
+            b1[f, own1 + i] = restrict2(pair, pad1) * 0.5
+    near_start(b1, s_b1, r_b1, True)
+
     near_wait(l1, s_l1, r_l1, False, distances=(1, 2, 3))
     first1 = 2 * me - own1
     width1 = 2 * own1 + 2
@@ -338,33 +398,16 @@
 
     each(1, width1 - 1, operator1)
 
-    halo_wait(0)
-    halo_wait(1)
-    each(half, cx, first0_c)
-    each(2 * cx, 2 * cx + half, first0_c)
-    each(cx - 1, 2 * cx + 1, functools.partial(first_sweeps, ua, c0, g0, size0))
-
-    for f in range(2):
-        for i in range(2):
-            p = cx + 2 * i
-            pair = (residue(ua, b0, e0, d0, size0, f, p, p + 1, p, p)
-                    + residue(ua, b0, e0, d0, size0, f, p + 1, p + 2, p + 1, p + 1))
-            b1[f, own1 + i] = restrict2(pair, pad1) * 0.5
-    near_start(b1, s_b1, r_b1, True)
-
     all_wait(l2, s_l2, r_l2, False)
     counts = [ns >> i for i in range(3)]
-    logs = l2
     for i in range(3):
         e, ie, d, q, g, c, u, w = coarse[i]
         size, pad, n = sizes[2 + i], pads[2 + i], counts[i]
         e[0] = jnp.zeros(pad, F32)
         e[n + 1] = jnp.zeros(pad, F32)
         for ref in (u, w):
-            for f in range(2):
-                ref[f, 0] = jnp.zeros(pad, F32)
-                ref[f, n + 1] = jnp.zeros(pad, F32)
-        source = l2 if i == 0 else None
+            ref[0] = jnp.zeros(pad, F32)
+            ref[n + 1] = jnp.zeros(pad, F32)
 
         def exps(p, e=e, ie=ie, size=size, pad=pad, n=n, i=i, d=d):
             if i == 0:
@@ -374,7 +417,7 @@
                 logk = restrict2(above[2 * p] + above[2 * p + 1], pad, 3) * 0.125
                 g_now = coarse[i][4]
                 g_now[p] = logk
-            ok = inside(pad, size, p, n - 1)
+            ok = inside(pad, size, p, n - 1, 2)
             e[p + 1] = jnp.where(ok, jnp.exp(0.5 * logk), 0.0)
             ie[p] = jnp.where(ok, jnp.exp(-0.5 * logk), 0.0)
 
@@ -385,8 +428,8 @@
 
         def ops(p, e=e, d=d, q=q, g=g, size=size, pad=pad, n=n):
             center = e[p + 1]
-            dd = diag_plane(center, e[p], e[p + 2], p, n - 1, size)
-            qq = jnp.where(inside(pad, size, p, n - 1), OMEGA / dd, 0.0)
+            dd = diag_plane(center, e[p], e[p + 2], p, n - 1, size, 2)
+            qq = jnp.where(inside(pad, size, p, n - 1, 2), OMEGA / dd, 0.0)
             d[p] = dd
             q[p] = qq
             g[p] = qq * center
@@ -401,42 +444,42 @@
     near_wait(b1, s_b1, r_b1, True, distances=(1,))
     each(own1 - 2, own1 + 4, first1_c)
     each(own1 - 1, own1 + 3, functools.partial(first_sweeps, va, c1, g1, size1))
-    for f in range(2):
-        pair = (residue(va, b1, e1, d1, size1, f, own1, own1, own1, own1)
-                + residue(va, b1, e1, d1, size1, f, own1 + 1, own1 + 1, own1 + 1, own1 + 1))
-        b2[f, pl.ds(me, 1)] = (restrict2(pair, pad2) * 0.5)[None]
-    all_start(b2, s_b2, r_b2, True)
-
-    halo_wait(2)
-    halo_wait(3)
-    each(0, half, first0_c)
-    each(2 * cx + half, 3 * cx, first0_c)
-    each(1, cx - 1, functools.partial(first_sweeps, ua, c0, g0, size0))
-    each(2 * cx + 1, 3 * cx - 1, functools.partial(first_sweeps, ua, c0, g0, size0))
+    pairs = [(residue(va, b1, e1, d1, size1, f, own1, own1, own1, own1)
+              + residue(va, b1, e1, d1, size1, f, own1 + 1, own1 + 1, own1 + 1, own1 + 1))
+             for f in range(2)]
+    side = [right_mul(pairs[f], pad2[1], lambda i, j, f=f: half_of(i) + f * size2[1] == j)
+            for f in range(2)]
+    b2[pl.ds(me, 1)] = (left_mul(side[0] + side[1], pad2[0], coarsen) * 0.5)[None]
+    all_start(b2, s_b2, r_b2, False)
+    halo_start(2)
+    halo_start(3)
+
     near_wait(b1, s_b1, r_b1, True, distances=(2, 3))
     each(own1 - 5, own1 - 2, first1_c)
     each(own1 + 4, own1 + 7, first1_c)
     each(own1 - 4, own1 - 1, functools.partial(first_sweeps, va, c1, g1, size1))
     each(own1 + 3, own1 + 6, functools.partial(first_sweeps, va, c1, g1, size1))
 
-    all_wait(b2, s_b2, r_b2, True)
+    all_wait(b2, s_b2, r_b2, False)
 
     def solve(i, source):
         e, ie, d, q, g, c, u, w = coarse[i]
         size, pad, n = sizes[2 + i], pads[2 + i], counts[i]
 
         def begin(p):
-            def one(f):
-                value = q[p] * source[f, p]
-                c[f, p] = value
-                u[f, p + 1] = value
-
-            both(one)
-
-        each(0, n, begin)
+            value = q[p] * source[p]
+            c[p] = value
+            u[p + 1] = value
+
+        each(0, n, begin, 8)
 
         def full(src, dst):
-            each(1, n + 1, lambda p: sweep(src, c, g, dst, size, p, p - 1, p - 1))
+            def one(p):
+                now = src[p]
+                total = src[p - 1] + src[p + 1] + nsum(now, size, 2)
+                dst[p] = (1.0 - OMEGA) * now + c[p - 1] + g[p - 1] * total
+
+            each(1, n + 1, one, 8)
 
         if i == 2:
             now, then = u, w
@@ -445,52 +488,54 @@
                 now, then = then, now
             return now
         full(u, w)
-        below = rest_source[i + 1]
+        below = (b3, b4)[i]
+
+        def rest_of(p):
+            now = w[p + 1]
+            total = w[p] + w[p + 2] + nsum(now, size, 2)
+            return source[p] + e[p + 1] * total - d[p] * now
 
         def down(p):
-            def one(f):
-                pair = (residue(w, source, e, d, size, f, 2 * p + 1, 2 * p + 1, 2 * p, 2 * p)
-                        + residue(w, source, e, d, size, f, 2 * p + 2, 2 * p + 2, 2 * p + 1, 2 * p + 1))
-                below[f, p] = restrict2(pair, pads[3 + i]) * 0.5
-
-            both(one)
-
-        each(0, counts[i + 1], down)
+            below[p] = restrict2(rest_of(2 * p) + rest_of(2 * p + 1), pads[3 + i]) * 0.5
+
+        each(0, counts[i + 1], down, 4)
         fix = solve(i + 1, below)
         fix_inv = coarse[i + 1][1]
 
         def up(p):
-            def one(f):
-                add = prolong2(fix[f, p + 1] * fix_inv[p], pad)
-                w[f, 2 * p + 1] = w[f, 2 * p + 1] + e[2 * p + 1] * add
-                w[f, 2 * p + 2] = w[f, 2 * p + 2] + e[2 * p + 2] * add
-
-            both(one)
-
-        each(0, counts[i + 1], up)
+            add = prolong2(fix[p + 1] * fix_inv[p], pad)
+            w[2 * p + 1] = w[2 * p + 1] + e[2 * p + 1] * add
+            w[2 * p + 2] = w[2 * p + 2] + e[2 * p + 2] * add
+
+        each(0, counts[i + 1], up, 4)
         full(w, u)
         full(u, w)
         return w
 
-    rest_source = [b2, coarse[1][6], coarse[2][6]]
-    rest_source = [b2, pv0, pv1]
     top = solve(0, b2)
     top_inv = coarse[0][1]
+    halo_pass(2)
+    halo_pass(3)
 
     def correct1(k):
         at = jnp.clip(me - 2 + k, 0, ns - 1)
         p = own1 - 4 + 2 * k
-
-        def one(f):
-            add = prolong2(top[f, at + 1] * top_inv[at], pad1)
+        rows = left_mul(top[at + 1] * top_inv[at], pad1[0], refine)
+        for f in range(2):
+            add = right_mul(rows, pad1[1], lambda i, j, f=f: i == f * size2[1] + half_of(j))
             va[f, p] = va[f, p] + e1[p] * add
             va[f, p + 1] = va[f, p + 1] + e1[p + 1] * add
-
-        both(one)
 
     each(0, 5, correct1)
     each(own1 - 3, own1 + 5, functools.partial(sweep, va, c1, g1, vb, size1))
     each(own1 - 2, own1 + 4, functools.partial(sweep, vb, c1, g1, va, size1))
+
+    halo_wait(2)
+    halo_wait(3)
+    each(0, half, first0_c)
+    each(2 * cx + half, 3 * cx, first0_c)
+    each(1, cx - 1, functools.partial(first_sweeps, ua, c0, g0, size0))
+    each(2 * cx + 1, 3 * cx - 1, functools.partial(first_sweeps, ua, c0, g0, size0))
 
     def correct0(f, l, planes):
         add = prolong2(va[f, l] * ie1[l], size0)
@@ -539,7 +584,8 @@
     by_z = jnp.where(iz > 0, by_z, 0.0)
     cells = plain + 0.5 * (by_y + roll(by_y, -1, 0) + by_z + roll(by_z, -1, 1))
     zy, zz = zone_ref.shape[1:]
-    zone = right_mul(left_mul(cells, zy, 0, 2, 3), zz, 2, 0, 3)
+    quarter = lambda i, j: jnp.right_shift(i, 2) == j
+    zone = right_mul(left_mul(cells, zy, quarter, 3), zz, quarter, 3)
     weight_sum = weight_ref[0]
     for w in range(1, weight_ref.shape[0]):
         weight_sum = weight_sum + weight_ref[w]
@@ -552,16 +598,12 @@
     zone_copy.start()
 
     for i in range(4):
-        way = halo[i][0]
-
-        @pl.when(in_range(me + way))
-        def _():
-            halo_copy(*halo[i], me + way).wait_send()
+        halo_sent(i)
 
     near_sent(l1, s_l1, r_l1, False)
     near_sent(b1, s_b1, r_b1, True)
     all_sent(l2, s_l2, r_l2, False)
-    all_sent(b2, s_b2, r_b2, True)
+    all_sent(b2, s_b2, r_b2, False)
     zone_copy.wait()
     zone_ref[0] = own_zone[...] + other_zone[...]
 
@@ -579,29 +621,30 @@
         vmem((2, wide) + p0, F32), vmem((wide + 2,) + p0, F32), vmem((wide,) + p0, F32),
         vmem((wide,) + p0, F32), vmem((wide,) + p0, F32), vmem((2, wide) + p0, F32),
         vmem((2, wide) + p0, F32), vmem((2, wide) + p0, F32), vmem((wide + 2,) + p0, F32),
-        vmem((wide + 2,) + p0, F32), vmem((2, ns // 2) + pads[3], F32),
+        vmem((wide + 2,) + p0, F32), vmem((ns // 2,) + pads[3], F32),
         vmem((2, near) + p1, F32), vmem((near,) + p1, F32), vmem((near,) + p1, F32),
         vmem((near,) + p1, F32), vmem((near,) + p1, F32), vmem((near,) + p1, F32),
         vmem((near,) + p1, F32), vmem((2, near) + p1, F32), vmem((2, near) + p1, F32),
-        vmem((2, near) + p1, F32), vmem((2, ns // 4) + pads[4], F32),
-        vmem((ns,) + p2, F32), vmem((2, ns) + p2, F32),
+        vmem((2, near) + p1, F32), vmem((ns // 4,) + pads[4], F32),
+        vmem((ns,) + p2, F32), vmem((ns,) + p2, F32),
     ]
     for i in range(3):
         n, pad = ns >> i, pads[2 + i]
         scratch += [vmem((n + 2,) + pad, F32), vmem((n,) + pad, F32), vmem((n,) + pad, F32),
-                    vmem((n,) + pad, F32), vmem((n,) + pad, F32), vmem((2, n) + pad, F32),
-                    vmem((2, n + 2) + pad, F32), vmem((2, n + 2) + pad, F32)]
+                    vmem((n,) + pad, F32), vmem((n,) + pad, F32), vmem((n,) + pad, F32),
+                    vmem((n + 2,) + pad, F32), vmem((n + 2,) + pad, F32)]
     zone = (ny // 4, nz // 4)
     scratch += [vmem(zone, F32), vmem(zone, F32)]
     spread = 2 * REACH + 1
-    scratch += [dma((4,)), dma((4,)), dma((spread,)), dma((spread,)), dma((spread,)), dma((spread,)),
+    scratch += [dma((8,)), dma((8,)), dma((2,)), dma((spread,)), dma((spread,)), dma((spread,)), dma((spread,)),
                 dma((ns,)), dma((ns,)), dma((ns,)), dma((ns,)), dma, dma]
     in_v, in_s = pl.BlockSpec(memory_space=vmem), pl.BlockSpec(memory_space=smem)
     field = jax.ShapeDtypeStruct((1, cx, ny, nz), F32)
     return pl.pallas_call(
         functools.partial(kernel, ns, sizes, pads),
         out_shape=(field, field, jax.ShapeDtypeStruct((1,) + zone, F32)),
-        in_specs=[in_s, in_s, in_v, in_s, in_s, in_v],
+        in_specs=[in_s, in_s, pl.BlockSpec(memory_space=pl.ANY), in_s, in_s,
+                  pl.BlockSpec(memory_space=pl.ANY)],
         out_specs=(in_v, in_v, in_v),
         scratch_shapes=scratch,
         compiler_params=pltpu.CompilerParams(

time: 70.7 us -> 46.5 us (0.66)
  Pallas kernels: 65.3 us -> 41 us
    pallas_call x1, Pallas kernels: 65.3 us -> 41 us  [body(): pl.pallas_call(functools.partial(kernel, ns, sizes, pads), out_shape=(fie...]
where the time goes in v2:
time: 46.5 us; the launch traced here: 46.3 us
  Pallas kernels  41 us (88%)
  local copies, waits for them, and re-layouts  3.91 us (8%)
  between operations  1.37 us (3%)
    pallas_call x1, Pallas kernels, body(): pl.pallas_call(functools.partial(kernel, ns, sizes, pads), out_shape=(fie...  41 us
    unnamed x13, local copies, waits for them, and re-layouts  3.91 us

profile of v2, /device:TPU:0, one launch (start us, length us, event | category | flops | bytes accessed | tf_op | source)
XLA Modules:
  0.0 46.3 jit_solution(15608043642376750682)
XLA Ops:
  0.6 0.0 copy-start.4
  0.6 0.0 copy-start.3
  0.7 0.0 copy-start.2
  1.3 0.0 copy-done.4
  1.3 0.0 copy-done.3
  1.4 0.0 copy-done.2
  1.4 0.0 copy-start
  1.4 0.9 %copy-done = f32[4,64,256]{2,1,0:T(8,128)S(1)} copy-done((f32[4,64,256]{2,1,0:T(8,128)S(1)}, f32[4,64,256]{2,1,0:T(8,128)}, u32[]{:S(2)}) %copy-start) | copy-done | bytes 262168
  2.3 0.0 copy-start.1
  2.3 0.9 %copy-done.1 = f32[4,64,256]{2,1,0:T(8,128)S(1)} copy-done((f32[4,64,256]{2,1,0:T(8,128)S(1)}, f32[4,64,256]{2,1,0:T(8,128)}, u32[]{:S(2)}) %copy-start.1) | copy-done | bytes 262168
  3.3 41.0 %shard_map.85 = (f32[1,4,64,256]{3,2,1,0:T(8,128)S(1)}, f32[1,4,64,256]{3,2,1,0:T(8,128)S(1)}, f32[1,16,64]{2,1,0:T(8,128)S(1)}) custom-call(s32[1]{0:T(128)S(6)} %copy.12.seed_ref, s32[2]{0:T(128)S(1)} %copy-done.2, f32[4,64,256]{2,1,0:T(8,128)S(1)} %copy-done, s32[8]{0:T(128)S(1)} %copy-done.3, f32[8]{0:T(128)S(1)} %copy-done.4, f32[4,64,256]{2,1,0:T(8,128)S(1)} %copy-done.1), custom_call_target="tpu_custom_call" | custom-call | tf_op jit(solution)/shard_map/pallas_call | solution.py:643
  44.3 0.7 %copy.13 = f32[1,4,64,256]{3,2,1,0:T(8,128)} copy(f32[1,4,64,256]{3,2,1,0:T(8,128)S(1)} %get-tuple-element.6) | data formatting | bytes 524288
  45.0 0.7 %copy.14 = f32[1,4,64,256]{3,2,1,0:T(8,128)} copy(f32[1,4,64,256]{3,2,1,0:T(8,128)S(1)} %get-tuple-element.7) | data formatting | bytes 524288
  45.7 0.6 %copy.15 = f32[1,16,64]{2,1,0:T(8,128)} copy(f32[1,16,64]{2,1,0:T(8,128)S(1)} %get-tuple-element.8) | data formatting | bytes 8192
Async XLA Ops:
  0.6 0.7 %copy-start.4 = (f32[8]{0:T(128)S(1)}, f32[8]{0:T(128)}, u32[]{:S(2)}) copy-start(f32[8]{0:T(128)} %rates_ref.1) | copy-start | bytes 100
  0.6 0.7 %copy-start.3 = (s32[8]{0:T(128)S(1)}, s32[8]{0:T(128)}, u32[]{:S(2)}) copy-start(s32[8]{0:T(128)} %cells_ref.1) | copy-start | bytes 100
  0.7 0.7 %copy-start.2 = (s32[2]{0:T(128)S(1)}, s32[2]{0:T(128)}, u32[]{:S(2)}) copy-start(s32[2]{0:T(128)} %weight_ref.1) | copy-start | bytes 28
  1.4 1.0 %copy-start = (f32[4,64,256]{2,1,0:T(8,128)S(1)}, f32[4,64,256]{2,1,0:T(8,128)}, u32[]{:S(2)}) copy-start(f32[4,64,256]{2,1,0:T(8,128)} %recharge_ref.1) | copy-start | bytes 786436
  2.3 0.9 %copy-start.1 = (f32[4,64,256]{2,1,0:T(8,128)S(1)}, f32[4,64,256]{2,1,0:T(8,128)}, u32[]{:S(2)}) copy-start(f32[4,64,256]{2,1,0:T(8,128)} %sens_ref.1) | copy-start | bytes 786436

commit v3 on v2

--- a/solution.py
+++ b/solution.py
@@ -118,12 +118,12 @@
 
 def kernel(ns, sizes, pads, seed_ref, weight_ref, recharge_ref, cells_ref, rates_ref, sens_ref,
            head_ref, adj_ref, zone_ref,
-           b0, e0, d0, q0, g0, c0, ua, ub, l0, ie0, b3,
+           b0, e0, d0, q0, g0, c0, ua, ub, ie0, b3,
            b1, l1, e1, ie1, d1, q1, g1, c1, va, vb, b4,
            l2, b2, *rest):
     coarse = [rest[8 * i: 8 * i + 8] for i in range(3)]
     own_zone, other_zone = rest[24:26]
-    s_halo, r_halo, s_in, s_l1, r_l1, s_b1, r_b1, s_l2, r_l2, s_b2, r_b2, s_z, r_z = rest[26:]
+    s_halo, r_halo, s_in, s_b1, r_b1, s_l2, r_l2, s_b2, r_b2, s_z, r_z = rest[26:]
     me = lax.axis_index("slab")
     node = lax.axis_index("node")
     size0, size1, size2 = sizes[:3]
@@ -150,7 +150,6 @@
         each(2 * cx, 3 * cx, lambda p: both(lambda f: b0.__setitem__((f, p), zero0)))
 
     def clear1(p):
-        l1[p] = zero1
         b1[0, p] = zero1
         b1[1, p] = zero1
 
@@ -289,24 +288,29 @@
     hashed_place = place * 747796405
     first0 = me * cx - cx
 
-    def logk_plane(p):
-        x_now = first0 - 1 + p
+    def logk_at(x_now):
         q = hashed_place + (x_now * (size0[0] * size0[1]) * 747796405 + seed_part)
         q = jnp.bitwise_xor(q, lax.shift_right_logical(q, jnp.full(size0, 15, jnp.int32)))
         q = q * 1274126177
         q = jnp.bitwise_xor(q, lax.shift_right_logical(q, jnp.full(size0, 13, jnp.int32)))
         low = jnp.bitwise_and(q, 65535)
-        logk = 3.0 * (low.astype(F32) / 65536.0) - 1.5
-        l0[p] = logk
+        return 3.0 * (low.astype(F32) / 65536.0) - 1.5
+
+    def logk_plane(p):
+        x_now = first0 - 1 + p
+        logk = logk_at(x_now)
         known = (x_now >= 0) & (x_now <= last0)
         e0[p] = jnp.where(known, jnp.exp(0.5 * logk), 0.0)
         ie0[p] = jnp.exp(-0.5 * logk)
 
     each(0, 3 * cx + 2, logk_plane)
-    for i in range(2):
-        pair = l0[cx + 1 + 2 * i] + l0[cx + 2 + 2 * i]
-        l1[own1 + i] = restrict2(pair, pad1, 3) * 0.125
-    near_start(l1, s_l1, r_l1, False)
+    first1 = 2 * me - own1
+
+    def logk1_plane(p):
+        x_now = 2 * (first1 + p)
+        l1[p] = restrict2(logk_at(x_now) + logk_at(x_now + 1), pad1, 3) * 0.125
+
+    each(own1, own1 + 2, logk1_plane)
     both_fields = right_mul(l1[own1] + l1[own1 + 1], pad2[1],
                             lambda i, j: half_of(i) == jnp.bitwise_and(j, size2[1] - 1), 3)
     l2[pl.ds(me, 1)] = (left_mul(both_fields, pad2[0], coarsen, 3) * 0.125)[None]
@@ -358,13 +362,17 @@
 
     each(cx, 2 * cx, first0_c)
 
+    each(0, own1, logk1_plane)
     halo_pass(0)
     halo_pass(1)
+    each(own1 + 2, 2 * own1 + 2, logk1_plane)
+    each(cx + 1, 2 * cx - 1, functools.partial(first_sweeps, ua, c0, g0, size0))
     halo_wait(0)
     halo_wait(1)
     each(half, cx, first0_c)
     each(2 * cx, 2 * cx + half, first0_c)
-    each(cx - 1, 2 * cx + 1, functools.partial(first_sweeps, ua, c0, g0, size0))
+    each(cx - 1, cx + 1, functools.partial(first_sweeps, ua, c0, g0, size0))
+    each(2 * cx - 1, 2 * cx + 1, functools.partial(first_sweeps, ua, c0, g0, size0))
 
     for f in range(2):
         for i in range(2):
@@ -374,8 +382,6 @@
             b1[f, own1 + i] = restrict2(pair, pad1) * 0.5
     near_start(b1, s_b1, r_b1, True)
 
-    near_wait(l1, s_l1, r_l1, False, distances=(1, 2, 3))
-    first1 = 2 * me - own1
     width1 = 2 * own1 + 2
 
     def exp1(p):
@@ -600,7 +606,6 @@
     for i in range(4):
         halo_sent(i)
 
-    near_sent(l1, s_l1, r_l1, False)
     near_sent(b1, s_b1, r_b1, True)
     all_sent(l2, s_l2, r_l2, False)
     all_sent(b2, s_b2, r_b2, False)
@@ -620,7 +625,7 @@
     scratch = [
         vmem((2, wide) + p0, F32), vmem((wide + 2,) + p0, F32), vmem((wide,) + p0, F32),
         vmem((wide,) + p0, F32), vmem((wide,) + p0, F32), vmem((2, wide) + p0, F32),
-        vmem((2, wide) + p0, F32), vmem((2, wide) + p0, F32), vmem((wide + 2,) + p0, F32),
+        vmem((2, wide) + p0, F32), vmem((2, wide) + p0, F32),
         vmem((wide + 2,) + p0, F32), vmem((ns // 2,) + pads[3], F32),
         vmem((2, near) + p1, F32), vmem((near,) + p1, F32), vmem((near,) + p1, F32),
         vmem((near,) + p1, F32), vmem((near,) + p1, F32), vmem((near,) + p1, F32),
@@ -636,7 +641,7 @@
     zone = (ny // 4, nz // 4)
     scratch += [vmem(zone, F32), vmem(zone, F32)]
     spread = 2 * REACH + 1
-    scratch += [dma((8,)), dma((8,)), dma((2,)), dma((spread,)), dma((spread,)), dma((spread,)), dma((spread,)),
+    scratch += [dma((8,)), dma((8,)), dma((2,)), dma((spread,)), dma((spread,)),
                 dma((ns,)), dma((ns,)), dma((ns,)), dma((ns,)), dma, dma]
     in_v, in_s = pl.BlockSpec(memory_space=vmem), pl.BlockSpec(memory_space=smem)
     field = jax.ShapeDtypeStruct((1, cx, ny, nz), F32)

time: 46.5 us -> 44.8 us (0.963)
  Pallas kernels: 41 us -> 39.3 us
    pallas_call x1, Pallas kernels: 41 us -> 39.3 us  [body(): pl.pallas_call(functools.partial(kernel, ns, sizes, pads), out_shape=(fie...]
where the time goes in v3:
time: 44.8 us; the launch traced here: 44.6 us
  Pallas kernels  39.3 us (88%)
  local copies, waits for them, and re-layouts  3.91 us (9%)
  between operations  1.37 us (3%)
    pallas_call x1, Pallas kernels, body(): pl.pallas_call(functools.partial(kernel, ns, sizes, pads), out_shape=(fie...  39.3 us
    unnamed x13, local copies, waits for them, and re-layouts  3.91 us

profile of v3, /device:TPU:0, one launch (start us, length us, event | category | flops | bytes accessed | tf_op | source)
XLA Modules:
  0.0 44.6 jit_solution(15157766402946595785)
XLA Ops:
  0.6 0.0 copy-start.4
  0.6 0.0 copy-start.3
  0.7 0.0 copy-start.2
  1.3 0.0 copy-done.4
  1.3 0.0 copy-done.3
  1.4 0.0 copy-done.2
  1.4 0.0 copy-start
  1.4 0.9 %copy-done = f32[4,64,256]{2,1,0:T(8,128)S(1)} copy-done((f32[4,64,256]{2,1,0:T(8,128)S(1)}, f32[4,64,256]{2,1,0:T(8,128)}, u32[]{:S(2)}) %copy-start) | copy-done | bytes 262168
  2.3 0.0 copy-start.1
  2.3 0.9 %copy-done.1 = f32[4,64,256]{2,1,0:T(8,128)S(1)} copy-done((f32[4,64,256]{2,1,0:T(8,128)S(1)}, f32[4,64,256]{2,1,0:T(8,128)}, u32[]{:S(2)}) %copy-start.1) | copy-done | bytes 262168
  3.3 39.3 %shard_map.85 = (f32[1,4,64,256]{3,2,1,0:T(8,128)S(1)}, f32[1,4,64,256]{3,2,1,0:T(8,128)S(1)}, f32[1,16,64]{2,1,0:T(8,128)S(1)}) custom-call(s32[1]{0:T(128)S(6)} %copy.12.seed_ref, s32[2]{0:T(128)S(1)} %copy-done.2, f32[4,64,256]{2,1,0:T(8,128)S(1)} %copy-done, s32[8]{0:T(128)S(1)} %copy-done.3, f32[8]{0:T(128)S(1)} %copy-done.4, f32[4,64,256]{2,1,0:T(8,128)S(1)} %copy-done.1), custom_call_target="tpu_custom_call" | custom-call | tf_op jit(solution)/shard_map/pallas_call | solution.py:648
  42.6 0.7 %copy.13 = f32[1,4,64,256]{3,2,1,0:T(8,128)} copy(f32[1,4,64,256]{3,2,1,0:T(8,128)S(1)} %get-tuple-element.6) | data formatting | bytes 524288
  43.3 0.7 %copy.14 = f32[1,4,64,256]{3,2,1,0:T(8,128)} copy(f32[1,4,64,256]{3,2,1,0:T(8,128)S(1)} %get-tuple-element.7) | data formatting | bytes 524288
  44.0 0.6 %copy.15 = f32[1,16,64]{2,1,0:T(8,128)} copy(f32[1,16,64]{2,1,0:T(8,128)S(1)} %get-tuple-element.8) | data formatting | bytes 8192
Async XLA Ops:
  0.6 0.7 %copy-start.4 = (f32[8]{0:T(128)S(1)}, f32[8]{0:T(128)}, u32[]{:S(2)}) copy-start(f32[8]{0:T(128)} %rates_ref.1) | copy-start | bytes 100
  0.6 0.7 %copy-start.3 = (s32[8]{0:T(128)S(1)}, s32[8]{0:T(128)}, u32[]{:S(2)}) copy-start(s32[8]{0:T(128)} %cells_ref.1) | copy-start | bytes 100
  0.7 0.7 %copy-start.2 = (s32[2]{0:T(128)S(1)}, s32[2]{0:T(128)}, u32[]{:S(2)}) copy-start(s32[2]{0:T(128)} %weight_ref.1) | copy-start | bytes 28
  1.4 1.0 %copy-start = (f32[4,64,256]{2,1,0:T(8,128)S(1)}, f32[4,64,256]{2,1,0:T(8,128)}, u32[]{:S(2)}) copy-start(f32[4,64,256]{2,1,0:T(8,128)} %recharge_ref.1) | copy-start | bytes 786436
  2.3 0.9 %copy-start.1 = (f32[4,64,256]{2,1,0:T(8,128)S(1)}, f32[4,64,256]{2,1,0:T(8,128)}, u32[]{:S(2)}) copy-start(f32[4,64,256]{2,1,0:T(8,128)} %sens_ref.1) | copy-start | bytes 786436

commit v4 on v3

--- a/solution.py
+++ b/solution.py
@@ -23,6 +23,9 @@
 def matrix(rows, cols, rule, dtype=jnp.bfloat16):
     shape = (rows, cols)
     return jnp.where(rule(iota(shape, 0), iota(shape, 1)), 1.0, 0.0).astype(dtype)
+
+
+KEPT = {}
 
 
 def half_of(i):
@@ -47,7 +50,8 @@
 
 
 def right_mul(x, cols, rule, terms=2):
-    m = matrix(x.shape[1], cols, rule)
+    m = KEPT.get((x.shape[1], cols, rule))
+    m = matrix(x.shape[1], cols, rule) if m is None else m
     out = None
     for part in split(x, terms):
         y = jnp.dot(part, m, preferred_element_type=F32)
@@ -56,7 +60,8 @@
 
 
 def left_mul(x, rows, rule, terms=2):
-    m = matrix(rows, x.shape[0], lambda i, j: rule(j, i))
+    m = KEPT.get((rule, rows, x.shape[0]))
+    m = matrix(rows, x.shape[0], lambda i, j: rule(j, i)) if m is None else m
     out = None
     for part in split(x, terms):
         y = jnp.dot(m, part, preferred_element_type=F32)
@@ -138,6 +143,14 @@
             src_ref=src, dst_ref=dst, send_sem=send, recv_sem=recv,
             device_id={"slab": slab}, device_id_type=pl.DeviceIdType.MESH)
 
+    KEPT.clear()
+    built = {}
+    for rule, fine, other in ((coarsen, 0, 1), (refine, 1, 0)):
+        (y, z), (rows, cols) = pads[fine], pads[other]
+        built[(z, cols, rule)] = matrix(z, cols, rule)
+        built[(rule, rows, y)] = matrix(rows, y, lambda i, j, rule=rule: rule(j, i))
+    KEPT.update(built)
+
     zero0 = jnp.zeros(size0, F32)
     zero1 = jnp.zeros(pad1, F32)
 
@@ -308,7 +321,7 @@
 
     def logk1_plane(p):
         x_now = 2 * (first1 + p)
-        l1[p] = restrict2(logk_at(x_now) + logk_at(x_now + 1), pad1, 3) * 0.125
+        l1[p] = restrict2(logk_at(x_now) + logk_at(x_now + 1), pad1) * 0.125
 
     each(own1, own1 + 2, logk1_plane)
     both_fields = right_mul(l1[own1] + l1[own1 + 1], pad2[1],
@@ -611,6 +624,7 @@
     all_sent(b2, s_b2, r_b2, False)
     zone_copy.wait()
     zone_ref[0] = own_zone[...] + other_zone[...]
+    KEPT.clear()
 
 
 def body(ns, field_seeds, quad_weight, recharge, well_cells, well_rates, sensitivity):

time: 44.8 us -> 44.4 us (level)
  Pallas kernels: 39.3 us -> 38.8 us
    pallas_call x1, Pallas kernels: 39.3 us -> 38.8 us  [body(): pl.pallas_call(functools.partial(kernel, ns, sizes, pads), out_shape=(fie...]
where the time goes in v4:
time: 44.4 us; the launch traced here: 44 us
  Pallas kernels  38.8 us (87%)
  local copies, waits for them, and re-layouts  3.91 us (9%)
  between operations  1.37 us (3%)
    pallas_call x1, Pallas kernels, body(): pl.pallas_call(functools.partial(kernel, ns, sizes, pads), out_shape=(fie...  38.8 us
    unnamed x13, local copies, waits for them, and re-layouts  3.91 us

profile of v4, /device:TPU:0, one launch (start us, length us, event | category | flops | bytes accessed | tf_op | source)
XLA Modules:
  0.0 44.0 jit_solution(13093928109361168493)
XLA Ops:
  0.6 0.0 copy-start.4
  0.6 0.0 copy-start.3
  0.7 0.0 copy-start.2
  1.3 0.0 copy-done.4
  1.3 0.0 copy-done.3
  1.4 0.0 copy-done.2
  1.4 0.0 copy-start
  1.4 0.9 %copy-done = f32[4,64,256]{2,1,0:T(8,128)S(1)} copy-done((f32[4,64,256]{2,1,0:T(8,128)S(1)}, f32[4,64,256]{2,1,0:T(8,128)}, u32[]{:S(2)}) %copy-start) | copy-done | bytes 262168
  2.3 0.0 copy-start.1
  2.3 0.9 %copy-done.1 = f32[4,64,256]{2,1,0:T(8,128)S(1)} copy-done((f32[4,64,256]{2,1,0:T(8,128)S(1)}, f32[4,64,256]{2,1,0:T(8,128)}, u32[]{:S(2)}) %copy-start.1) | copy-done | bytes 262168
  3.3 38.8 %shard_map.85 = (f32[1,4,64,256]{3,2,1,0:T(8,128)S(1)}, f32[1,4,64,256]{3,2,1,0:T(8,128)S(1)}, f32[1,16,64]{2,1,0:T(8,128)S(1)}) custom-call(s32[1]{0:T(128)S(6)} %copy.12.seed_ref, s32[2]{0:T(128)S(1)} %copy-done.2, f32[4,64,256]{2,1,0:T(8,128)S(1)} %copy-done, s32[8]{0:T(128)S(1)} %copy-done.3, f32[8]{0:T(128)S(1)} %copy-done.4, f32[4,64,256]{2,1,0:T(8,128)S(1)} %copy-done.1), custom_call_target="tpu_custom_call" | custom-call | tf_op jit(solution)/shard_map/pallas_call | solution.py:662
  42.0 0.7 %copy.13 = f32[1,4,64,256]{3,2,1,0:T(8,128)} copy(f32[1,4,64,256]{3,2,1,0:T(8,128)S(1)} %get-tuple-element.6) | data formatting | bytes 524288
  42.7 0.7 %copy.14 = f32[1,4,64,256]{3,2,1,0:T(8,128)} copy(f32[1,4,64,256]{3,2,1,0:T(8,128)S(1)} %get-tuple-element.7) | data formatting | bytes 524288
  43.4 0.6 %copy.15 = f32[1,16,64]{2,1,0:T(8,128)} copy(f32[1,16,64]{2,1,0:T(8,128)S(1)} %get-tuple-element.8) | data formatting | bytes 8192
Async XLA Ops:
  0.6 0.7 %copy-start.4 = (f32[8]{0:T(128)S(1)}, f32[8]{0:T(128)}, u32[]{:S(2)}) copy-start(f32[8]{0:T(128)} %rates_ref.1) | copy-start | bytes 100
  0.6 0.7 %copy-start.3 = (s32[8]{0:T(128)S(1)}, s32[8]{0:T(128)}, u32[]{:S(2)}) copy-start(s32[8]{0:T(128)} %cells_ref.1) | copy-start | bytes 100
  0.7 0.7 %copy-start.2 = (s32[2]{0:T(128)S(1)}, s32[2]{0:T(128)}, u32[]{:S(2)}) copy-start(s32[2]{0:T(128)} %weight_ref.1) | copy-start | bytes 28
  1.4 1.0 %copy-start = (f32[4,64,256]{2,1,0:T(8,128)S(1)}, f32[4,64,256]{2,1,0:T(8,128)}, u32[]{:S(2)}) copy-start(f32[4,64,256]{2,1,0:T(8,128)} %recharge_ref.1) | copy-start | bytes 786436
  2.3 0.9 %copy-start.1 = (f32[4,64,256]{2,1,0:T(8,128)S(1)}, f32[4,64,256]{2,1,0:T(8,128)}, u32[]{:S(2)}) copy-start(f32[4,64,256]{2,1,0:T(8,128)} %sens_ref.1) | copy-start | bytes 786436
